TPU v7x, 32 devices: a whole 2x2x4 slice. The times are simulated.
32 devices in a mesh: rep: 8 (over z, y), gx: 2 (over x), gy: 2 (over core).
Axes of the slice: x: 2, y: 2, z: 4, core: 2. Of those that a mesh axis runs over, the one named last changes fastest.
Arguments:
- particle_descriptors: bfloat16 [8, 4, 4, 128, 128], P('rep', 'gx', 'gy'), may hold values from -6 to 6
- particle_locations_all: float32 [8, 3, 4, 4, 128], P('rep', None, 'gx', 'gy'), may hold values from 0 to 4, as said below
- earlier_jitter: float32 [8, 3, 4, 4, 128], P('rep', None, 'gx', 'gy'), may hold values from -6 to 6
- later_jitter: float32 [8, 3, 4, 4, 128], P('rep', None, 'gx', 'gy'), may hold values from -6 to 6
- adjacent_tile_slots: int32 [4, 4, 6], P('gx', 'gy'), may hold values from -1 to 15, as said below
- thermal_levels: float32 [8], replicated, may hold values from 0.5 to 2
- heat_slot_of_copy: int32 [8], P('rep'), may hold values from 0 to 7, as said below
- partner_choice: int32 [8], replicated, may hold values from 0 to 7, as said below
- normalizer_gain: float32 [128], replicated, may hold values from 0.25 to 1.75
- query_lookup_matrix: bfloat16 [128, 384], replicated, may hold values from -0.5 to 0.5
- message_output_matrix: bfloat16 [128, 128], replicated, may hold values from -0.5 to 0.5
- lookup_charge_map: bfloat16 [128], replicated, may hold values from -0.5 to 0.5
- attention_head_falloff: float32 [8], replicated, may hold values from 0.5 to 8
- attention_head_weight: float32 [8], replicated, may hold values from -4 to 4
Outputs:
- interval_descriptors: bfloat16 [8, 4, 4, 128, 128], P('rep', 'gx', 'gy')
- interval_locations: float32 [8, 3, 4, 4, 128], P('rep', None, 'gx', 'gy')
- later_pulls: float32 [8, 3, 4, 4, 128], P('rep', None, 'gx', 'gy')
Inputs may be any that keep to these rules, and one draw needn't show every extreme that they name: `adjacent_tile_slots`: each tile's first slot names the tile itself; the others name distinct tiles of the 3 x 3 block of tiles around it that lie inside the grid, as row-major indices into the device's block of tiles extended by one tile on each side (4 columns); -1 marks an empty slot, and empty slots come last. `heat_slot_of_copy`: A permutation. `partner_choice`: an involution: each replica takes its own configuration or that of the replica whose temperature slot is next to its own. `particle_locations_all`: for a bead of the tile at grid position (a, b) the first coordinate lies in [a, a + 1], the second in [b, b + 1], the third in [0, 1].
All inputs are finite; a program needn't handle non-finite values.
Results may differ from a plain program's by a relative error of at most 0.0091.
Values may be sent and summed in bfloat16 or wider, within the bound.
A program may use at most 64 MiB of HBM per device.

v0:
```python
import math

import jax
import jax.numpy as jnp
from jax import lax
from jax.sharding import PartitionSpec as P

NORM_EPS = 1e-05
DURATION_DELTA = 0.1
JITTER_SIZE = 0.05
MESSAGE_SCALE = 1.0 / 32.0
FORCE_SCALE = 1.0 / 16.0


def with_halo(cells, sides, width):
    for axis, dim in sides:
        count = lax.axis_size(axis)
        ends = count - 1
        head = lax.slice_in_dim(cells, 0, width, axis=dim)
        tail = lax.slice_in_dim(cells, cells.shape[dim] - width, cells.shape[dim], axis=dim)
        cells = jnp.concatenate(
            [
                lax.ppermute(tail, axis, [(i, (i + 1) % count) for i in range(ends)]),
                cells,
                lax.ppermute(head, axis, [((i + 1) % count, i) for i in range(ends)]),
            ],
            axis=dim,
        )
    return cells


def layer_norm(latent_vector, normalizer_gain):
    values = latent_vector.astype(jnp.float32)
    center = jnp.mean(values, axis=-1, keepdims=True)
    spread = jnp.mean((values - center) ** 2, axis=-1, keepdims=True)
    return ((values - center) * lax.rsqrt(spread + NORM_EPS) * normalizer_gain).astype(jnp.bfloat16)


def tile_terms(
    query_rows,
    own_coords,
    keyval,
    probe_values,
    near_coords,
    occupied_flags,
    attention_head_falloff,
    attention_head_weight,
):
    bead_count, feature_count = query_rows.shape
    head_count = attention_head_falloff.shape[0]
    head_size = feature_count // head_count
    slot_count = keyval.shape[0]
    queries = query_rows.reshape(bead_count, head_count, head_size)
    keys_heads = keyval[..., :feature_count].reshape(slot_count, bead_count, head_count, head_size)
    values_heads = keyval[..., feature_count:].reshape(
        slot_count, bead_count, head_count, head_size
    )
    logits = jnp.einsum("ihd,njhd->hinj", queries, keys_heads, preferred_element_type=jnp.float32)
    offsets = own_coords[:, :, None, None] - near_coords[:, None, :, :]
    squared = jnp.sum(offsets * offsets, axis=0)
    radius = jnp.sqrt(squared)
    envelope = jnp.where(radius < 1.0, 0.5 * (jnp.cos(jnp.pi * radius) + 1.0), 0.0)
    envelope = envelope * occupied_flags.astype(jnp.float32)[None, :, None]
    scores = (
        jax.nn.silu(logits / math.sqrt(head_size))
        * envelope[None]
        * jnp.exp(-attention_head_falloff[:, None, None, None] * squared[None])
    )
    message = (
        jnp.einsum(
            "hinj,njhd->ihd",
            scores.astype(jnp.bfloat16),
            values_heads,
            preferred_element_type=jnp.float32,
        )
        * MESSAGE_SCALE
    )
    message = message.reshape(bead_count, feature_count).astype(jnp.bfloat16)
    mixing = jnp.sum(attention_head_weight[:, None, None, None] * scores, axis=0)
    particle_pulls = (
        jnp.sum(offsets * (mixing * probe_values[None, :, :])[None], axis=(2, 3)) * FORCE_SCALE
    )
    return (message, particle_pulls)


def propagate_copy(
    latent_vector,
    particle_locations,
    stochastic_jolts,
    copy_heat_level,
    adjacent_tile_slots,
    network_weights,
):
    (
        normalizer_gain,
        query_lookup_matrix,
        message_output_matrix,
        lookup_charge_map,
        attention_head_falloff,
        attention_head_weight,
    ) = network_weights
    tiles_x, tiles_y, tile_beads, feature_count = latent_vector.shape
    tile_total = tiles_x * tiles_y
    slot_count = adjacent_tile_slots.shape[2]
    normed = layer_norm(latent_vector, normalizer_gain)
    flat_normed = normed.reshape(-1, feature_count)
    projected = jnp.dot(
        flat_normed, query_lookup_matrix, preferred_element_type=jnp.float32
    ).astype(jnp.bfloat16)
    query_rows = projected[:, :feature_count].reshape(tile_total, tile_beads, feature_count)
    local_keyval = projected[:, feature_count:].reshape(
        tiles_x, tiles_y, tile_beads, 2 * feature_count
    )
    extended = with_halo(local_keyval, (("gx", 0), ("gy", 1)), 1)
    keyval = extended.reshape(-1, tile_beads, 2 * feature_count)
    probe_values = jnp.dot(
        keyval[..., :feature_count].reshape(-1, feature_count),
        lookup_charge_map,
        preferred_element_type=jnp.float32,
    ).reshape(-1, tile_beads)
    near_coords = with_halo(particle_locations, (("gx", 1), ("gy", 2)), 1).reshape(
        3, -1, tile_beads
    )
    own_coords = particle_locations.reshape(3, tile_total, tile_beads).transpose(1, 0, 2)
    slot_table = adjacent_tile_slots.reshape(tile_total, slot_count)
    occupied_flags = slot_table >= 0
    clipped = jnp.maximum(slot_table, 0)

    def per_tile(tile_item):
        tile_query, tile_coords, tile_slots, tile_present = tile_item
        return tile_terms(
            tile_query,
            tile_coords,
            keyval[tile_slots],
            probe_values[tile_slots],
            near_coords[:, tile_slots],
            tile_present,
            attention_head_falloff,
            attention_head_weight,
        )

    message, particle_pulls = lax.map(per_tile, (query_rows, own_coords, clipped, occupied_flags))
    mixed = jnp.dot(
        message.reshape(-1, feature_count),
        message_output_matrix,
        preferred_element_type=jnp.float32,
    ).reshape(latent_vector.shape)
    revised_latent = (latent_vector.astype(jnp.float32) + mixed).astype(jnp.bfloat16)
    particle_pulls = particle_pulls.transpose(1, 0, 2).reshape(particle_locations.shape)
    moved_locations = (
        particle_locations
        + DURATION_DELTA * particle_pulls
        + JITTER_SIZE * jnp.sqrt(copy_heat_level) * stochastic_jolts
    )
    return (revised_latent, moved_locations, particle_pulls)


def per_device(
    particle_descriptors,
    particle_locations_all,
    earlier_jitter,
    later_jitter,
    adjacent_tile_slots,
    thermal_levels,
    heat_slot_of_copy,
    partner_choice,
    normalizer_gain,
    query_lookup_matrix,
    message_output_matrix,
    lookup_charge_map,
    attention_head_falloff,
    attention_head_weight,
):
    network_weights = (
        normalizer_gain,
        query_lookup_matrix,
        message_output_matrix,
        lookup_charge_map,
        attention_head_falloff,
        attention_head_weight,
    )
    replicas = thermal_levels.shape[0]
    copy_orderings = jnp.arange(replicas, dtype=jnp.int32)
    copy_heat_level = jnp.sum(
        jnp.where(copy_orderings == heat_slot_of_copy[0], thermal_levels, 0.0)
    )
    starting_latent, starting_locations, ignored_output = propagate_copy(
        particle_descriptors[0],
        particle_locations_all[0],
        earlier_jitter[0],
        copy_heat_level,
        adjacent_tile_slots,
        network_weights,
    )
    tiles_x, tiles_y, tile_beads, feature_count = starting_latent.shape
    tile_total = tiles_x * tiles_y
    piece_beads = tile_beads // replicas
    spread_hidden = lax.all_to_all(
        starting_latent.reshape(tile_total, replicas, piece_beads * feature_count),
        "rep",
        split_axis=1,
        concat_axis=1,
        tiled=True,
    )
    routed_hidden = lax.all_to_all(
        jnp.take(spread_hidden, partner_choice, axis=1),
        "rep",
        split_axis=1,
        concat_axis=1,
        tiled=True,
    )
    traded_latent = routed_hidden.reshape(starting_latent.shape)
    spread_coords = lax.all_to_all(
        starting_locations.reshape(3 * tile_total, replicas, piece_beads),
        "rep",
        split_axis=1,
        concat_axis=1,
        tiled=True,
    )
    routed_coords = lax.all_to_all(
        jnp.take(spread_coords, partner_choice, axis=1),
        "rep",
        split_axis=1,
        concat_axis=1,
        tiled=True,
    )
    traded_locations = routed_coords.reshape(starting_locations.shape)
    revised_latent, moved_locations, particle_pulls = propagate_copy(
        traded_latent,
        traded_locations,
        later_jitter[0],
        copy_heat_level,
        adjacent_tile_slots,
        network_weights,
    )
    return (revised_latent[None], moved_locations[None], particle_pulls[None])


def solution(mesh):
    in_specs = (
        P("rep", "gx", "gy", None, None),
        P("rep", None, "gx", "gy", None),
        P("rep", None, "gx", "gy", None),
        P("rep", None, "gx", "gy", None),
        P("gx", "gy", None),
        P(),
        P("rep"),
        P(),
        P(),
        P(),
        P(),
        P(),
        P(),
        P(),
    )
    out_specs = (
        P("rep", "gx", "gy", None, None),
        P("rep", None, "gx", "gy", None),
        P("rep", None, "gx", "gy", None),
    )
    return jax.shard_map(
        per_device, mesh=mesh, in_specs=in_specs, out_specs=out_specs, check_vma=False
    )
```

profile of v0, /device:TPU:0, one launch (start us, length us, event | category | flops | bytes accessed | tf_op | source)
XLA Modules:
  0.0 152.6 jit_solution(779146749758944164)
XLA Ops:
  1.5 4.8 %collective-permute-start.4 = (f32[3,1,2,128]{3,2,1,0:T(2,128)S(1)}, f32[3,1,2,128]{3,2,1,0:T(2,128)S(1)}, u32[]{:S(2)}, u32[]{:S(2)}) collective-permute-start(f32[3,1,2,128]{3,2,1,0:T(2,128)S(1)} %get-tuple-element.525), channel_id=1, source_target_pairs={{0,2},{1,3},{4,6},{5,7},{8,10},{9,11},{12,14},{13,15},{16,18},{17,... | collective-permute-start | bytes 9224 | tf_op jit(solution)/shard_map/ppermute | solution.py:23
  6.3 1.3 collective-permute-start.5
  7.6 1.0 convert_reduce_fusion
  8.6 1.1 fusion.45
  9.8 1.1 fusion.43
  11.2 1.3 collective-permute-start.1
  12.5 4.6 %collective-permute-start = (bf16[1,2,128,256]{3,2,1,0:T(8,128)(2,1)S(1)}, bf16[1,2,128,256]{3,2,1,0:T(8,128)(2,1)S(1)}, u32[]{:S(2)}, u32[]{:S(2)}) collective-permute-start(bf16[1,2,128,256]{3,2,1,0:T(8,128)(2,1)S(1)} %bitcast.244), channel_id=1, source_target_pairs={{0,2},{1,3},{4,6},{5,7},{8,10},{9,11},{12,14},{13,15},{16,18},{17,... | collective-permute-start | bytes 393224 | tf_op jit(solution)/shard_map/ppermute | solution.py:23
  19.2 1.3 collective-permute-start.6
  20.5 1.3 collective-permute-start.7
  22.0 3.0 %collective-permute-start.2 = (bf16[4,1,128,256]{3,2,1,0:T(8,128)(2,1)S(1)}, bf16[4,1,128,256]{3,2,1,0:T(8,128)(2,1)S(1)}, u32[]{:S(2)}, u32[]{:S(2)}) collective-permute-start(bf16[4,1,128,256]{3,2,1,0:T(8,128)(2,1)S(1)} %get-tuple-element.513), channel_id=1, source_target_pairs={{0,1},{2,3},{4,5},{6,7},{8,9},{10,11},{12,13},{14,15},{16,17},{18,... | collective-permute-start | bytes 786440 | tf_op jit(solution)/shard_map/ppermute | solution.py:23
  25.0 1.3 collective-permute-start.3
  26.7 1.8 %collective-permute-done.3 = bf16[4,1,128,256]{3,2,1,0:T(8,128)(2,1)S(1)} collective-permute-done((bf16[4,1,128,256]{3,2,1,0:T(8,128)(2,1)S(1)}, bf16[4,1,128,256]{3,2,1,0:T(8,128)(2,1)S(1)}, u32[]{:S(2)}, u32[]{:S(2)}) %collective-permute-start.3) | collective-permute-done | bytes 262176 | tf_op jit(solution)/shard_map/ppermute | solution.py:25
  28.9 27.2 %while.28 = (s32[]{:T(128)}, bf16[4,128,128]{1,2,0:T(8,128)(2,1)S(1)}, f32[4,3,128]{2,1,0:T(4,128)S(1)}, s32[4,6]{1,0:T(4,128)S(1)}, bf16[16,128,256]{2,1,0:T(8,...) while((s32[]{:T(128)}, ...), condition=%wide.region_6.7_spmd, body=%wide.region_2.6_spmd.sunk | while | flops 61277208 | bytes 9780131 | solution.py:142
  31.5 1.4 select_multiply_fusion.4
  32.9 1.9 %multiply_reduce_fusion.5 = (f32[128,6,128]{2,0,1:T(8,128)S(1)}, bf16[8,128,6,128]{3,1,2,0:T(8,128)(2,1)S(1)}) fusion(f32[8]{0:T(128)S(1)} %get-tuple-element.725, f32[128,6,128]{2,0,1:T(8,128)S(1)} %fusion.97, f32[8]{0:T(128)S(1)} %bitcast.259, f32[128,6,128]{2,0,1:T(8,128)S(1)} %select_multiply_fusion.4, bf16[128,8,16,1]{0,2,3,1:T(8,128)(2,1)S(1)} %bitcast.229, ...), kind=kOutput, calls=%fused_computation.8.clone.1 | convolution fusion | flops 33718272 | bytes 2981952 | tf_op jit(solution)/shard_map/while/body/eval_jaxpr/ihd,njhd->hinj/dot_general | solution.py:58
  38.3 1.4 select_multiply_fusion.4
  39.7 1.9 %multiply_reduce_fusion.5 = (f32[128,6,128]{2,0,1:T(8,128)S(1)}, bf16[8,128,6,128]{3,1,2,0:T(8,128)(2,1)S(1)}) fusion(f32[8]{0:T(128)S(1)} %get-tuple-element.725, f32[128,6,128]{2,0,1:T(8,128)S(1)} %fusion.97, f32[8]{0:T(128)S(1)} %bitcast.259, f32[128,6,128]{2,0,1:T(8,128)S(1)} %select_multiply_fusion.4, bf16[128,8,16,1]{0,2,3,1:T(8,128)(2,1)S(1)} %bitcast.229, ...), kind=kOutput, calls=%fused_computation.8.clone.1 | convolution fusion | flops 33718272 | bytes 2981952 | tf_op jit(solution)/shard_map/while/body/eval_jaxpr/ihd,njhd->hinj/dot_general | solution.py:58
  45.1 1.4 select_multiply_fusion.4
  46.6 1.9 %multiply_reduce_fusion.5 = (f32[128,6,128]{2,0,1:T(8,128)S(1)}, bf16[8,128,6,128]{3,1,2,0:T(8,128)(2,1)S(1)}) fusion(f32[8]{0:T(128)S(1)} %get-tuple-element.725, f32[128,6,128]{2,0,1:T(8,128)S(1)} %fusion.97, f32[8]{0:T(128)S(1)} %bitcast.259, f32[128,6,128]{2,0,1:T(8,128)S(1)} %select_multiply_fusion.4, bf16[128,8,16,1]{0,2,3,1:T(8,128)(2,1)S(1)} %bitcast.229, ...), kind=kOutput, calls=%fused_computation.8.clone.1 | convolution fusion | flops 33718272 | bytes 2981952 | tf_op jit(solution)/shard_map/while/body/eval_jaxpr/ihd,njhd->hinj/dot_general | solution.py:58
  51.9 1.4 select_multiply_fusion.4
  53.4 1.9 %multiply_reduce_fusion.5 = (f32[128,6,128]{2,0,1:T(8,128)S(1)}, bf16[8,128,6,128]{3,1,2,0:T(8,128)(2,1)S(1)}) fusion(f32[8]{0:T(128)S(1)} %get-tuple-element.725, f32[128,6,128]{2,0,1:T(8,128)S(1)} %fusion.97, f32[8]{0:T(128)S(1)} %bitcast.259, f32[128,6,128]{2,0,1:T(8,128)S(1)} %select_multiply_fusion.4, bf16[128,8,16,1]{0,2,3,1:T(8,128)(2,1)S(1)} %bitcast.229, ...), kind=kOutput, calls=%fused_computation.8.clone.1 | convolution fusion | flops 33718272 | bytes 2981952 | tf_op jit(solution)/shard_map/while/body/eval_jaxpr/ihd,njhd->hinj/dot_general | solution.py:58
  57.0 5.8 %all-to-all-start.2 = ((f32[8,1,192]{2,1,0:T(1,128)}), f32[8,1,192]{2,1,0:T(1,128)S(1)}, u32[]{:S(2)}, u32[]{:S(2)}) async-start(f32[8,1,192]{2,1,0:T(1,128)} %reshape.471), calls=%async_computation.2 | async-start | bytes 16384 | tf_op jit(solution)/shard_map/all_to_all | solution.py:213
  62.9 6.5 %all-to-all-done.2 = f32[8,1,192]{2,1,0:T(1,128)S(1)} async-done(((f32[8,1,192]{2,1,0:T(1,128)}), f32[8,1,192]{2,1,0:T(1,128)S(1)}, u32[]{:S(2)}, u32[]{:S(2)}) %all-to-all-start.2) | async-done | bytes 6176 | tf_op jit(solution)/shard_map/all_to_all | solution.py:213
  72.0 3.3 %all-to-all-start.3 = ((f32[8,1,192]{2,1,0:T(1,128)}), f32[8,1,192]{2,1,0:T(1,128)S(1)}, u32[]{:S(2)}, u32[]{:S(2)}) async-start(f32[8,1,192]{2,1,0:T(1,128)} %reshape.473), calls=%async_computation.3 | async-start | bytes 16384 | tf_op jit(solution)/shard_map/all_to_all | solution.py:220
  76.4 5.4 %all-to-all-done.3 = f32[8,1,192]{2,1,0:T(1,128)S(1)} async-done(((f32[8,1,192]{2,1,0:T(1,128)}), f32[8,1,192]{2,1,0:T(1,128)S(1)}, u32[]{:S(2)}, u32[]{:S(2)}) %all-to-all-start.3) | async-done | bytes 6176 | tf_op jit(solution)/shard_map/all_to_all | solution.py:220
  81.8 3.4 %all-to-all-start = ((bf16[4,8,2048]{2,0,1:T(4,128)(2,1)}), bf16[4,8,2048]{2,0,1:T(4,128)(2,1)S(1)}, u32[]{:S(2)}, u32[]{:S(2)}) async-start(bf16[4,8,2048]{2,0,1:T(4,128)(2,1)} %copy.171), calls=%async_computation | async-start | bytes 262144 | tf_op jit(solution)/shard_map/all_to_all | solution.py:198
  86.0 6.4 %all-to-all-done = bf16[4,8,2048]{2,0,1:T(4,128)(2,1)S(1)} async-done(((bf16[4,8,2048]{2,0,1:T(4,128)(2,1)}), bf16[4,8,2048]{2,0,1:T(4,128)(2,1)S(1)}, u32[]{:S(2)}, u32[]{:S(2)}) %all-to-all-start) | async-done | bytes 131104 | tf_op jit(solution)/shard_map/all_to_all | solution.py:198
  93.9 3.4 %all-to-all-start.1 = ((bf16[4,8,2048]{2,0,1:T(4,128)(2,1)}), bf16[4,8,2048]{2,0,1:T(4,128)(2,1)S(1)}, u32[]{:S(2)}, u32[]{:S(2)}) async-start(bf16[4,8,2048]{2,0,1:T(4,128)(2,1)} %select_bitcast_fusion), calls=%async_computation.1 | async-start | bytes 262144 | tf_op jit(solution)/shard_map/all_to_all | solution.py:205
  97.3 1.3 collective-permute-start.12
  98.6 1.3 collective-permute-start.13
  99.9 4.6 %all-to-all-done.1 = bf16[4,8,2048]{2,0,1:T(4,128)(2,1)S(1)} async-done(((bf16[4,8,2048]{2,0,1:T(4,128)(2,1)}), bf16[4,8,2048]{2,0,1:T(4,128)(2,1)S(1)}, u32[]{:S(2)}, u32[]{:S(2)}) %all-to-all-start.1) | async-done | bytes 131104 | tf_op jit(solution)/shard_map/all_to_all | solution.py:205
  105.6 1.3 collective-permute-start.9
  106.9 4.6 %collective-permute-start.8 = (bf16[1,2,128,256]{3,2,1,0:T(8,128)(2,1)S(1)}, bf16[1,2,128,256]{3,2,1,0:T(8,128)(2,1)S(1)}, u32[]{:S(2)}, u32[]{:S(2)}) collective-permute-start(bf16[1,2,128,256]{3,2,1,0:T(8,128)(2,1)S(1)} %bitcast.246), channel_id=1, source_target_pairs={{0,2},{1,3},{4,6},{5,7},{8,10},{9,11},{12,14},{13,15},{16,18},{17,... | collective-permute-start | bytes 393224 | tf_op jit(solution)/shard_map/ppermute | solution.py:23
  112.4 1.5 collective-permute-done.8
  114.0 1.3 collective-permute-start.10
  115.3 1.3 collective-permute-start.11
  116.7 3.0 %collective-permute-start.14 = (f32[3,4,1,128]{3,2,1,0:T(1,128)S(1)}, f32[3,4,1,128]{3,2,1,0:T(1,128)S(1)}, u32[]{:S(2)}, u32[]{:S(2)}) collective-permute-start(f32[3,4,1,128]{3,2,1,0:T(1,128)S(1)} %get-tuple-element.519), channel_id=1, source_target_pairs={{0,1},{2,3},{4,5},{6,7},{8,9},{10,11},{12,13},{14,15},{16,17},{18,... | collective-permute-start | bytes 18440 | tf_op jit(solution)/shard_map/ppermute | solution.py:23
  119.7 1.5 collective-permute-start.15
  121.4 1.4 collective-permute-done.15
  123.7 27.3 %while.29 = (s32[]{:T(128)}, bf16[4,128,128]{1,2,0:T(8,128)(2,1)S(1)}, f32[4,3,128]{2,1,0:T(4,128)S(1)}, s32[4,6]{1,0:T(4,128)S(1)}, bf16[16,128,256]{2,1,0:T(8,...) while((s32[]{:T(128)}, ...), condition=%wide.region_14.15_spmd, body=%wide.region_10.14_spmd.sunk | while | flops 61277208 | bytes 9783203 | solution.py:142
  126.3 1.4 select_multiply_fusion.5
  127.7 1.9 %multiply_reduce_fusion.6 = (f32[128,6,128]{2,0,1:T(8,128)S(1)}, bf16[8,128,6,128]{3,1,2,0:T(8,128)(2,1)S(1)}) fusion(f32[8]{0:T(128)S(1)} %get-tuple-element.764, f32[128,6,128]{2,0,1:T(8,128)S(1)} %fusion.106, f32[8]{0:T(128)S(1)} %bitcast.260, f32[128,6,128]{2,0,1:T(8,128)S(1)} %select_multiply_fusion.5, ...), kind=kOutput, calls=%fused_computation.33.clone.1 | convolution fusion | flops 33718272 | bytes 2981952 | tf_op jit(solution)/shard_map/while/body/eval_jaxpr/ihd,njhd->hinj/dot_general | solution.py:58
  133.1 1.4 select_multiply_fusion.5
  134.6 1.9 %multiply_reduce_fusion.6 = (f32[128,6,128]{2,0,1:T(8,128)S(1)}, bf16[8,128,6,128]{3,1,2,0:T(8,128)(2,1)S(1)}) fusion(f32[8]{0:T(128)S(1)} %get-tuple-element.764, f32[128,6,128]{2,0,1:T(8,128)S(1)} %fusion.106, f32[8]{0:T(128)S(1)} %bitcast.260, f32[128,6,128]{2,0,1:T(8,128)S(1)} %select_multiply_fusion.5, ...), kind=kOutput, calls=%fused_computation.33.clone.1 | convolution fusion | flops 33718272 | bytes 2981952 | tf_op jit(solution)/shard_map/while/body/eval_jaxpr/ihd,njhd->hinj/dot_general | solution.py:58
  140.0 1.4 select_multiply_fusion.5
  141.4 1.9 %multiply_reduce_fusion.6 = (f32[128,6,128]{2,0,1:T(8,128)S(1)}, bf16[8,128,6,128]{3,1,2,0:T(8,128)(2,1)S(1)}) fusion(f32[8]{0:T(128)S(1)} %get-tuple-element.764, f32[128,6,128]{2,0,1:T(8,128)S(1)} %fusion.106, f32[8]{0:T(128)S(1)} %bitcast.260, f32[128,6,128]{2,0,1:T(8,128)S(1)} %select_multiply_fusion.5, ...), kind=kOutput, calls=%fused_computation.33.clone.1 | convolution fusion | flops 33718272 | bytes 2981952 | tf_op jit(solution)/shard_map/while/body/eval_jaxpr/ihd,njhd->hinj/dot_general | solution.py:58
  146.8 1.4 select_multiply_fusion.5
  148.2 1.9 %multiply_reduce_fusion.6 = (f32[128,6,128]{2,0,1:T(8,128)S(1)}, bf16[8,128,6,128]{3,1,2,0:T(8,128)(2,1)S(1)}) fusion(f32[8]{0:T(128)S(1)} %get-tuple-element.764, f32[128,6,128]{2,0,1:T(8,128)S(1)} %fusion.106, f32[8]{0:T(128)S(1)} %bitcast.260, f32[128,6,128]{2,0,1:T(8,128)S(1)} %select_multiply_fusion.5, ...), kind=kOutput, calls=%fused_computation.33.clone.1 | convolution fusion | flops 33718272 | bytes 2981952 | tf_op jit(solution)/shard_map/while/body/eval_jaxpr/ihd,njhd->hinj/dot_general | solution.py:58
  (282 shorter events, 40.6 us)
Async XLA Ops:
  0.6 10.3 %copy-start = (bf16[128,384]{1,0:T(8,128)(2,1)S(1)}, bf16[128,384]{1,0:T(8,128)(2,1)}, u32[]{:S(2)}) copy-start(bf16[128,384]{1,0:T(8,128)(2,1)} %param.27) | copy-start | bytes 294916
  0.6 18.5 %copy-start.4 = (f32[1,3,2,2,128]{4,3,2,1,0:T(2,128)S(1)}, f32[1,3,2,2,128]{4,3,2,1,0:T(2,128)}, u32[]{:S(2)}) copy-start(f32[1,3,2,2,128]{4,3,2,1,0:T(2,128)} %param.19) | copy-start | bytes 18436
  0.7 16.4 %copy-start.7 = (s32[2,2,6]{2,1,0:T(2,128)S(1)}, s32[2,2,6]{2,1,0:T(2,128)}, u32[]{:S(2)}) copy-start(s32[2,2,6]{2,1,0:T(2,128)} %param.22) | copy-start | bytes 292
  0.7 17.1 %copy-start.11 = (f32[8]{0:T(128)S(1)}, f32[8]{0:T(128)}, u32[]{:S(2)}) copy-start(f32[8]{0:T(128)} %param.23) | copy-start | bytes 100
  0.7 18.4 %copy-start.12 = (s32[8]{0:T(128)S(1)}, s32[8]{0:T(128)}, u32[]{:S(2)}) copy-start(s32[8]{0:T(128)} %param.25) | copy-start | bytes 100
  0.7 18.4 %copy-start.8 = (f32[1,3,2,2,128]{4,3,2,1,0:T(2,128)S(1)}, f32[1,3,2,2,128]{4,3,2,1,0:T(2,128)}, u32[]{:S(2)}) copy-start(f32[1,3,2,2,128]{4,3,2,1,0:T(2,128)} %param.20) | copy-start | bytes 18436
  1.5 17.7 %collective-permute-start.4 = (f32[3,1,2,128]{3,2,1,0:T(2,128)S(1)}, f32[3,1,2,128]{3,2,1,0:T(2,128)S(1)}, u32[]{:S(2)}, u32[]{:S(2)}) collective-permute-start(f32[3,1,2,128]{3,2,1,0:T(2,128)S(1)} %get-tuple-element.525), channel_id=1, source_target_pairs={{0,2},{1,3},{4,6},{5,7},{8,10},{9,11},{12,14},{13,15},{16,18},{17,... | collective-permute-start | bytes 9224 | tf_op jit(solution)/shard_map/ppermute | solution.py:23
  6.3 12.9 %collective-permute-start.5 = (f32[3,1,2,128]{3,2,1,0:T(2,128)S(1)}, f32[3,1,2,128]{3,2,1,0:T(2,128)S(1)}, u32[]{:S(2)}, u32[]{:S(2)}) collective-permute-start(f32[3,1,2,128]{3,2,1,0:T(2,128)S(1)} %get-tuple-element.526), channel_id=1, source_target_pairs={{2,0},{3,1},{6,4},{7,5},{10,8},{11,9},{14,12},{15,13},{18,16},{19,... | collective-permute-start | bytes 9224 | tf_op jit(solution)/shard_map/ppermute | solution.py:25
  11.2 15.3 %copy-start.2 = (bf16[512,384]{1,0:T(8,128)(2,1)}, bf16[512,384]{1,0:T(8,128)(2,1)S(1)}, u32[]{:S(2)}) copy-start(bf16[512,384]{1,0:T(8,128)(2,1)S(1)} %convolution_convert_fusion.1) | copy-start | bytes 1179652
  11.2 15.1 %copy-start.13 = (f32[8]{0:T(128)S(1)}, f32[8]{0:T(128)}, u32[]{:S(2)}) copy-start(f32[8]{0:T(128)} %param.30) | copy-start | bytes 100
  11.2 10.6 %collective-permute-start.1 = (bf16[1,2,128,256]{3,2,1,0:T(8,128)(2,1)S(1)}, bf16[1,2,128,256]{3,2,1,0:T(8,128)(2,1)S(1)}, u32[]{:S(2)}, u32[]{:S(2)}) collective-permute-start(bf16[1,2,128,256]{3,2,1,0:T(8,128)(2,1)S(1)} %bitcast.245), channel_id=1, source_target_pairs={{2,0},{3,1},{6,4},{7,5},{10,8},{11,9},{14,12},{15,13},{18,16},{19,... | collective-permute-start | bytes 393224 | tf_op jit(solution)/shard_map/ppermute | solution.py:25
  12.5 9.3 %collective-permute-start = (bf16[1,2,128,256]{3,2,1,0:T(8,128)(2,1)S(1)}, bf16[1,2,128,256]{3,2,1,0:T(8,128)(2,1)S(1)}, u32[]{:S(2)}, u32[]{:S(2)}) collective-permute-start(bf16[1,2,128,256]{3,2,1,0:T(8,128)(2,1)S(1)} %bitcast.244), channel_id=1, source_target_pairs={{0,2},{1,3},{4,6},{5,7},{8,10},{9,11},{12,14},{13,15},{16,18},{17,... | collective-permute-start | bytes 393224 | tf_op jit(solution)/shard_map/ppermute | solution.py:23
  19.2 7.4 %collective-permute-start.6 = (f32[3,4,1,128]{3,2,1,0:T(1,128)S(1)}, f32[3,4,1,128]{3,2,1,0:T(1,128)S(1)}, u32[]{:S(2)}, u32[]{:S(2)}) collective-permute-start(f32[3,4,1,128]{3,2,1,0:T(1,128)S(1)} %get-tuple-element.521), channel_id=1, source_target_pairs={{0,1},{2,3},{4,5},{6,7},{8,9},{10,11},{12,13},{14,15},{16,17},{18,... | collective-permute-start | bytes 18440 | tf_op jit(solution)/shard_map/ppermute | solution.py:23
  20.5 6.1 %collective-permute-start.7 = (f32[3,4,1,128]{3,2,1,0:T(1,128)S(1)}, f32[3,4,1,128]{3,2,1,0:T(1,128)S(1)}, u32[]{:S(2)}, u32[]{:S(2)}) collective-permute-start(f32[3,4,1,128]{3,2,1,0:T(1,128)S(1)} %get-tuple-element.522), channel_id=1, source_target_pairs={{1,0},{3,2},{5,4},{7,6},{9,8},{11,10},{13,12},{15,14},{17,16},{19,... | collective-permute-start | bytes 18440 | tf_op jit(solution)/shard_map/ppermute | solution.py:25
  21.9 6.7 %copy-start.14 = (bf16[128]{0:T(256)(128)(2,1)S(1)}, bf16[128]{0:T(256)(128)(2,1)}, u32[]{:S(2)}) copy-start(bf16[128]{0:T(256)(128)(2,1)} %param.29) | copy-start | bytes 772
  22.0 4.7 %collective-permute-start.2 = (bf16[4,1,128,256]{3,2,1,0:T(8,128)(2,1)S(1)}, bf16[4,1,128,256]{3,2,1,0:T(8,128)(2,1)S(1)}, u32[]{:S(2)}, u32[]{:S(2)}) collective-permute-start(bf16[4,1,128,256]{3,2,1,0:T(8,128)(2,1)S(1)} %get-tuple-element.513), channel_id=1, source_target_pairs={{0,1},{2,3},{4,5},{6,7},{8,9},{10,11},{12,13},{14,15},{16,17},{18,... | collective-permute-start | bytes 786440 | tf_op jit(solution)/shard_map/ppermute | solution.py:23
  25.0 3.4 %collective-permute-start.3 = (bf16[4,1,128,256]{3,2,1,0:T(8,128)(2,1)S(1)}, bf16[4,1,128,256]{3,2,1,0:T(8,128)(2,1)S(1)}, u32[]{:S(2)}, u32[]{:S(2)}) collective-permute-start(bf16[4,1,128,256]{3,2,1,0:T(8,128)(2,1)S(1)} %get-tuple-element.514), channel_id=1, source_target_pairs={{1,0},{3,2},{5,4},{7,6},{9,8},{11,10},{13,12},{15,14},{17,16},{19,... | collective-permute-start | bytes 786440 | tf_op jit(solution)/shard_map/ppermute | solution.py:25
  26.5 2.4 %slice-start.1 = ((bf16[512,384]{1,0:T(8,128)(2,1)}), bf16[512,128]{1,0:T(8,128)(2,1)S(1)}, s32[]{:S(2)}) async-start(bf16[512,384]{1,0:T(8,128)(2,1)} %copy-done.2), calls=%async_computation.5 | async-start | bytes 262144 | tf_op jit(solution)/shard_map/slice | solution.py:110
  26.5 2.4 %copy-start.15 = (f32[8]{0:T(128)S(1)}, f32[8]{0:T(128)}, u32[]{:S(2)}) copy-start(f32[8]{0:T(128)} %param.31) | copy-start | bytes 100
  28.9 46.4 %copy-start.3 = (bf16[1,2,2,128,128]{4,3,2,1,0:T(8,128)(2,1)S(1)}, bf16[1,2,2,128,128]{4,3,2,1,0:T(8,128)(2,1)}, u32[]{:S(2)}) copy-start(bf16[1,2,2,128,128]{4,3,2,1,0:T(8,128)(2,1)} %param.18) | copy-start | bytes 393220
  28.9 46.4 %copy-start.5 = (bf16[128,128]{1,0:T(8,128)(2,1)S(1)}, bf16[128,128]{1,0:T(8,128)(2,1)}, u32[]{:S(2)}) copy-start(bf16[128,128]{1,0:T(8,128)(2,1)} %param.28) | copy-start | bytes 98308
  57.0 12.4 %all-to-all-start.2 = ((f32[8,1,192]{2,1,0:T(1,128)}), f32[8,1,192]{2,1,0:T(1,128)S(1)}, u32[]{:S(2)}, u32[]{:S(2)}) async-start(f32[8,1,192]{2,1,0:T(1,128)} %reshape.471), calls=%async_computation.2 | async-start | bytes 16384 | tf_op jit(solution)/shard_map/all_to_all | solution.py:213
  72.0 9.8 %all-to-all-start.3 = ((f32[8,1,192]{2,1,0:T(1,128)}), f32[8,1,192]{2,1,0:T(1,128)S(1)}, u32[]{:S(2)}, u32[]{:S(2)}) async-start(f32[8,1,192]{2,1,0:T(1,128)} %reshape.473), calls=%async_computation.3 | async-start | bytes 16384 | tf_op jit(solution)/shard_map/all_to_all | solution.py:220
  81.8 10.7 %all-to-all-start = ((bf16[4,8,2048]{2,0,1:T(4,128)(2,1)}), bf16[4,8,2048]{2,0,1:T(4,128)(2,1)S(1)}, u32[]{:S(2)}, u32[]{:S(2)}) async-start(bf16[4,8,2048]{2,0,1:T(4,128)(2,1)} %copy.171), calls=%async_computation | async-start | bytes 262144 | tf_op jit(solution)/shard_map/all_to_all | solution.py:198
  85.2 20.0 %copy-start.10 = (f32[128]{0:T(128)S(1)}, f32[128]{0:T(128)}, u32[]{:S(2)}) copy-start(f32[128]{0:T(128)} %param.26) | copy-start | bytes 1540
  93.9 10.7 %all-to-all-start.1 = ((bf16[4,8,2048]{2,0,1:T(4,128)(2,1)}), bf16[4,8,2048]{2,0,1:T(4,128)(2,1)S(1)}, u32[]{:S(2)}, u32[]{:S(2)}) async-start(bf16[4,8,2048]{2,0,1:T(4,128)(2,1)} %select_bitcast_fusion), calls=%async_computation.1 | async-start | bytes 262144 | tf_op jit(solution)/shard_map/all_to_all | solution.py:205
  97.3 2.6 %collective-permute-start.12 = (f32[3,1,2,128]{3,2,1,0:T(2,128)S(1)}, f32[3,1,2,128]{3,2,1,0:T(2,128)S(1)}, u32[]{:S(2)}, u32[]{:S(2)}) collective-permute-start(f32[3,1,2,128]{3,2,1,0:T(2,128)S(1)} %get-tuple-element.524), channel_id=1, source_target_pairs={{0,2},{1,3},{4,6},{5,7},{8,10},{9,11},{12,14},{13,15},{16,18},{17,... | collective-permute-start | bytes 9224 | tf_op jit(solution)/shard_map/ppermute | solution.py:23
  98.6 12.9 %collective-permute-start.13 = (f32[3,1,2,128]{3,2,1,0:T(2,128)S(1)}, f32[3,1,2,128]{3,2,1,0:T(2,128)S(1)}, u32[]{:S(2)}, u32[]{:S(2)}) collective-permute-start(f32[3,1,2,128]{3,2,1,0:T(2,128)S(1)} %get-tuple-element.523), channel_id=1, source_target_pairs={{2,0},{3,1},{6,4},{7,5},{10,8},{11,9},{14,12},{15,13},{18,16},{19,... | collective-permute-start | bytes 9224 | tf_op jit(solution)/shard_map/ppermute | solution.py:25
  105.5 17.3 %copy-start.1 = (bf16[512,384]{1,0:T(8,128)(2,1)}, bf16[512,384]{1,0:T(8,128)(2,1)S(1)}, u32[]{:S(2)}) copy-start(bf16[512,384]{1,0:T(8,128)(2,1)S(1)} %convolution_convert_fusion) | copy-start | bytes 1179652
  105.6 6.9 %collective-permute-start.9 = (bf16[1,2,128,256]{3,2,1,0:T(8,128)(2,1)S(1)}, bf16[1,2,128,256]{3,2,1,0:T(8,128)(2,1)S(1)}, u32[]{:S(2)}, u32[]{:S(2)}) collective-permute-start(bf16[1,2,128,256]{3,2,1,0:T(8,128)(2,1)S(1)} %bitcast.247), channel_id=1, source_target_pairs={{2,0},{3,1},{6,4},{7,5},{10,8},{11,9},{14,12},{15,13},{18,16},{19,... | collective-permute-start | bytes 393224 | tf_op jit(solution)/shard_map/ppermute | solution.py:25
  106.9 7.1 %collective-permute-start.8 = (bf16[1,2,128,256]{3,2,1,0:T(8,128)(2,1)S(1)}, bf16[1,2,128,256]{3,2,1,0:T(8,128)(2,1)S(1)}, u32[]{:S(2)}, u32[]{:S(2)}) collective-permute-start(bf16[1,2,128,256]{3,2,1,0:T(8,128)(2,1)S(1)} %bitcast.246), channel_id=1, source_target_pairs={{0,2},{1,3},{4,6},{5,7},{8,10},{9,11},{12,14},{13,15},{16,18},{17,... | collective-permute-start | bytes 393224 | tf_op jit(solution)/shard_map/ppermute | solution.py:23
  114.0 8.8 %collective-permute-start.10 = (bf16[4,1,128,256]{3,2,1,0:T(8,128)(2,1)S(1)}, bf16[4,1,128,256]{3,2,1,0:T(8,128)(2,1)S(1)}, u32[]{:S(2)}, u32[]{:S(2)}) collective-permute-start(bf16[4,1,128,256]{3,2,1,0:T(8,128)(2,1)S(1)} %get-tuple-element.511), channel_id=1, source_target_pairs={{0,1},{2,3},{4,5},{6,7},{8,9},{10,11},{12,13},{14,15},{16,17},{18,... | collective-permute-start | bytes 786440 | tf_op jit(solution)/shard_map/ppermute | solution.py:23
  115.3 7.5 %collective-permute-start.11 = (bf16[4,1,128,256]{3,2,1,0:T(8,128)(2,1)S(1)}, bf16[4,1,128,256]{3,2,1,0:T(8,128)(2,1)S(1)}, u32[]{:S(2)}, u32[]{:S(2)}) collective-permute-start(bf16[4,1,128,256]{3,2,1,0:T(8,128)(2,1)S(1)} %get-tuple-element.512), channel_id=1, source_target_pairs={{1,0},{3,2},{5,4},{7,6},{9,8},{11,10},{13,12},{15,14},{17,16},{19,... | collective-permute-start | bytes 786440 | tf_op jit(solution)/shard_map/ppermute | solution.py:25
  116.7 4.7 %collective-permute-start.14 = (f32[3,4,1,128]{3,2,1,0:T(1,128)S(1)}, f32[3,4,1,128]{3,2,1,0:T(1,128)S(1)}, u32[]{:S(2)}, u32[]{:S(2)}) collective-permute-start(f32[3,4,1,128]{3,2,1,0:T(1,128)S(1)} %get-tuple-element.519), channel_id=1, source_target_pairs={{0,1},{2,3},{4,5},{6,7},{8,9},{10,11},{12,13},{14,15},{16,17},{18,... | collective-permute-start | bytes 18440 | tf_op jit(solution)/shard_map/ppermute | solution.py:23
  119.7 3.1 %collective-permute-start.15 = (f32[3,4,1,128]{3,2,1,0:T(1,128)S(1)}, f32[3,4,1,128]{3,2,1,0:T(1,128)S(1)}, u32[]{:S(2)}, u32[]{:S(2)}) collective-permute-start(f32[3,4,1,128]{3,2,1,0:T(1,128)S(1)} %get-tuple-element.520), channel_id=1, source_target_pairs={{1,0},{3,2},{5,4},{7,6},{9,8},{11,10},{13,12},{15,14},{17,16},{19,... | collective-permute-start | bytes 18440 | tf_op jit(solution)/shard_map/ppermute | solution.py:25
  122.8 0.9 slice-start
  123.7 28.2 %copy-start.9 = (f32[1,3,2,2,128]{4,3,2,1,0:T(2,128)S(1)}, f32[1,3,2,2,128]{4,3,2,1,0:T(2,128)}, u32[]{:S(2)}) copy-start(f32[1,3,2,2,128]{4,3,2,1,0:T(2,128)} %param.21) | copy-start | bytes 18436
  151.1 1.5 copy-start.6
where the time goes:
time: 153 us
  starting transfers between devices  50.3 us (33%)
  waiting for transfers between devices  28.6 us (19%)
  local copies, waits for them, and re-layouts  24.8 us (16%)
  other arithmetic  23.2 us (15%)
  matrix products  21.8 us (14%)
  between operations  2.89 us (2%)
    ppermute x8, starting transfers between devices, with_halo(): lax.ppermute(tail, axis, [(i, (i + 1) % count) for i in range(ends)])  23.9 us
    dot_general x8, matrix products, tile_terms(): jnp.einsum('ihd,njhd->hinj', queries, keys_heads, preferred_element_type=...  15.6 us
    mul x8, other arithmetic, tile_terms(): envelope = envelope * occupied_flags.astype(jnp.float32)[None, :, None]  11.3 us
    ppermute x8, starting transfers between devices, with_halo(): lax.ppermute(head, axis, [((i + 1) % count, i) for i in range(ends)])  10.5 us
    all_to_all x1, waiting for transfers between devices, per_device(): lax.all_to_all(starting_locations.reshape(3 * tile_total, replicas, piece...  6.51 us
    all_to_all x1, waiting for transfers between devices, per_device(): lax.all_to_all(starting_latent.reshape(tile_total, replicas, piece_beads...  6.39 us
    all_to_all x1, starting transfers between devices, per_device(): lax.all_to_all(starting_locations.reshape(3 * tile_total, replicas, piece...  5.84 us
    all_to_all x1, waiting for transfers between devices, per_device(): lax.all_to_all(jnp.take(spread_coords, partner_choice, axis=1), 'rep', sp...  5.38 us
  transfers between devices with their start and end apart: 20, of which 8 were waited for; matrix products, arithmetic and copies ran while one was open for 5% of the time, Pallas kernels for 0%

commit v1 on v0

v1 whole, which is shorter than its diff:
```python
import functools
import math

import jax
import jax.numpy as jnp
from jax import lax
from jax.experimental import pallas as pl
from jax.experimental.pallas import tpu as pltpu
from jax.sharding import PartitionSpec as P

NORM_EPS = 1e-05
DURATION_DELTA = 0.1
JITTER_SIZE = 0.05
MESSAGE_SCALE = 1.0 / 32.0
FORCE_SCALE = 1.0 / 16.0
LOG2E = math.log2(math.e)


def window_coefficients(degree):
    import numpy as np

    nodes = 0.5 - 0.5 * np.cos(np.pi * (np.arange(64) + 0.5) / 64)
    target = np.cos(0.5 * np.pi * np.sqrt(nodes)) / (1.0 - nodes)
    return [float(c) for c in np.polyfit(nodes, target, degree)]


WINDOW = window_coefficients(4)


def project(h, gain_row, weight):
    values = h.astype(jnp.float32)
    center = jnp.mean(values, axis=-1, keepdims=True)
    centred = values - center
    spread = jnp.mean(centred * centred, axis=-1, keepdims=True)
    normed = (centred * lax.rsqrt(spread + NORM_EPS) * gain_row).astype(jnp.bfloat16)
    return jnp.dot(normed, weight, preferred_element_type=jnp.float32).astype(jnp.bfloat16)


def tall(block):
    rows, lanes = block.shape
    return jnp.concatenate([block, jnp.zeros((lanes - rows, lanes), block.dtype)], axis=0)


def prepare_tile(t, h, pos, gain_row, weight, charge, k_ref, rhs_ref):
    feats = h.shape[1]
    proj = project(h, gain_row, weight)
    keys = proj[:, feats : 2 * feats]
    k_ref[t] = keys
    rhs_ref[t, :, :feats] = proj[:, 2 * feats :]
    probe = lax.dot_general(
        charge, keys, (((1,), (1,)), ((), ())), preferred_element_type=jnp.float32
    )
    rows = probe * pos
    high = rows.astype(jnp.bfloat16).astype(jnp.float32)
    columns = tall(jnp.concatenate([high, rows - high], axis=0)).T
    rhs_ref[t, :, feats:] = columns.astype(jnp.bfloat16)
    return proj[:, :feats]


def attend_tile(i, own, q, h, pos, noise, scale, slots, k_ref, rhs_ref, pos_ref, s_ref,
                falloff, mixing, out_weight):
    beads, feats = q.shape
    heads = falloff.shape[0]
    head_size = feats // heads
    slot_count = slots.shape[1]
    lane = lax.broadcasted_iota(jnp.int32, (beads, feats), 1) // head_size
    zero = jnp.zeros_like(q)
    stacked = jnp.concatenate([jnp.where(lane == e, q, zero) for e in range(heads)], axis=0)
    columns = tall(pos).T
    where, present = [], []
    for n in range(slot_count):
        slot = slots[i, n]
        present.append((slot >= 0).astype(jnp.float32))
        where.append(jnp.where(slot >= 0, slot, own))
    for first in range(0, slot_count, 2):
        pair = (first, first + 1)
        keys = jnp.concatenate([k_ref[where[n]] for n in pair], axis=0)
        logits = lax.dot_general(
            stacked, keys, (((1,), (1,)), ((), ())), preferred_element_type=jnp.float32
        )
        near = jnp.concatenate([pos_ref[where[n]] for n in pair], axis=1)
        occupied = jnp.concatenate(
            [jnp.full((1, beads), present[n], jnp.float32) for n in pair], axis=1
        )
        squared = None
        for c in range(3):
            offset = columns[:, c : c + 1] - near[c : c + 1, :]
            squared = offset * offset if squared is None else squared + offset * offset
        squared = jnp.minimum(squared, 1.0)
        window = jnp.full_like(squared, WINDOW[0])
        for coefficient in WINDOW[1:]:
            window = window * squared + coefficient
        window = window * (1.0 - squared)
        window = window * window * occupied
        for e in range(heads):
            half = logits[e * beads : (e + 1) * beads]
            act = half + half * jnp.tanh(half)
            score = act * (window * jnp.exp2(squared * (falloff[e] * -LOG2E)))
            s_ref[e * beads : (e + 1) * beads, first * beads : (first + 2) * beads] = score.astype(
                jnp.bfloat16
            )
    rhs = jnp.concatenate([rhs_ref[where[n]] for n in range(slot_count)], axis=0)
    sums = jnp.dot(s_ref[...], rhs, preferred_element_type=jnp.float32)
    message = jnp.zeros((beads, feats), jnp.float32)
    pulls = jnp.zeros((beads, feats), jnp.float32)
    for e in range(heads):
        part = sums[e * beads : (e + 1) * beads]
        message = jnp.where(lane == e, part[:, :feats], message)
        pulls = pulls + mixing[e] * part[:, feats:]
    message = (message * MESSAGE_SCALE).astype(jnp.bfloat16)
    mixed = jnp.dot(message, out_weight, preferred_element_type=jnp.float32)
    updated = (h.astype(jnp.float32) + mixed).astype(jnp.bfloat16)
    turned = pulls.T
    turned = turned[0:8] + turned[8:16]
    force = (pos * turned[3:4] - turned) * FORCE_SCALE
    moved = pos + DURATION_DELTA * force + (JITTER_SIZE * scale) * noise
    return updated, moved, force


def step_kernel(dims, h_ref, pos_ref, noise_ref, slots, heat, falloff, mixing, gain, weight,
                out_weight, charge, h_out, moved_out, force_out, k_ref, rhs_ref, q_ref, s_ref):
    tx, ty = dims
    for t in range((tx + 2) * (ty + 2)):
        q = prepare_tile(t, h_ref[t], pos_ref[t], gain[...], weight[...], charge[...], k_ref, rhs_ref)
        row, col = t // (ty + 2) - 1, t % (ty + 2) - 1
        if 0 <= row < tx and 0 <= col < ty:
            q_ref[row * ty + col] = q * jnp.bfloat16(0.125)

    def body(i, carry):
        own = (i // ty + 1) * (ty + 2) + lax.rem(i, ty) + 1
        updated, moved, force = attend_tile(
            i, own, q_ref[i], h_ref[own], pos_ref[own], noise_ref[i], jnp.sqrt(heat[0:1, 0:1]), slots,
            k_ref, rhs_ref, pos_ref, s_ref, falloff, mixing, out_weight[...])
        h_out[i] = updated
        moved_out[i] = moved
        force_out[i] = force
        return carry

    lax.fori_loop(0, tx * ty, body, 0)


def run_step(h_ext, pos_ext, noise, slots, heat, params, dims):
    gain, weight, out_weight, charge, falloff, mixing = params
    tx, ty = dims
    tiles, ext = tx * ty, (tx + 2) * (ty + 2)
    beads, feats = h_ext.shape[1:]
    heads = falloff.shape[0]
    vmem = pl.BlockSpec(memory_space=pltpu.VMEM)
    smem = pl.BlockSpec(memory_space=pltpu.SMEM)
    return pl.pallas_call(
        functools.partial(step_kernel, dims),
        out_shape=(
            jax.ShapeDtypeStruct((tiles, beads, feats), jnp.bfloat16),
            jax.ShapeDtypeStruct((tiles, 8, beads), jnp.float32),
            jax.ShapeDtypeStruct((tiles, 8, beads), jnp.float32),
        ),
        in_specs=[vmem, vmem, vmem, smem, vmem, smem, smem, vmem, vmem, vmem, vmem],
        out_specs=(vmem, vmem, vmem),
        scratch_shapes=[
            pltpu.VMEM((ext, beads, feats), jnp.bfloat16),
            pltpu.VMEM((ext, beads, 2 * feats), jnp.bfloat16),
            pltpu.VMEM((tiles, beads, feats), jnp.bfloat16),
            pltpu.VMEM((heads * beads, slots.shape[1] * beads), jnp.bfloat16),
        ],
        compiler_params=pltpu.CompilerParams(vmem_limit_bytes=40 * 2**20),
    )(h_ext, pos_ext, noise, slots, heat, falloff, mixing, gain, weight, out_weight, charge)


def with_halo(cells, sides, width):
    for axis, dim in sides:
        count = lax.axis_size(axis)
        ends = count - 1
        head = lax.slice_in_dim(cells, 0, width, axis=dim)
        tail = lax.slice_in_dim(cells, cells.shape[dim] - width, cells.shape[dim], axis=dim)
        cells = jnp.concatenate(
            [
                lax.ppermute(tail, axis, [(i, (i + 1) % count) for i in range(ends)]),
                cells,
                lax.ppermute(head, axis, [((i + 1) % count, i) for i in range(ends)]),
            ],
            axis=dim,
        )
    return cells


def as_rows(coords, fill):
    rows = coords.reshape(3, -1, coords.shape[-1]).transpose(1, 0, 2)
    one = jnp.full_like(rows[:, :1], fill)
    return jnp.concatenate([rows, one, jnp.zeros_like(rows), one * 0], axis=1)


def from_rows(rows, shape):
    return rows[:, :3].transpose(1, 0, 2).reshape(shape)


def per_device(
    particle_descriptors,
    particle_locations_all,
    earlier_jitter,
    later_jitter,
    adjacent_tile_slots,
    thermal_levels,
    heat_slot_of_copy,
    partner_choice,
    normalizer_gain,
    query_lookup_matrix,
    message_output_matrix,
    lookup_charge_map,
    attention_head_falloff,
    attention_head_weight,
):
    feats = normalizer_gain.shape[0]
    params = (
        normalizer_gain.reshape(1, feats),
        query_lookup_matrix,
        message_output_matrix,
        jnp.broadcast_to(lookup_charge_map[None], (8, feats)),
        attention_head_falloff,
        attention_head_weight,
    )
    replicas = thermal_levels.shape[0]
    heat = thermal_levels[heat_slot_of_copy[0]].reshape(1, 1)
    tx, ty = particle_descriptors.shape[1:3]
    slots = adjacent_tile_slots.reshape(tx * ty, -1)

    def step(h, p, noise):
        h_ext = with_halo(h, (("gx", 0), ("gy", 1)), 1)
        p_ext = with_halo(p, (("gx", 1), ("gy", 2)), 1)
        updated, moved, force = run_step(
            h_ext.reshape((-1,) + h.shape[2:]), as_rows(p_ext, 1.0), as_rows(noise, 0.0), slots,
            heat, params, (tx, ty))
        return updated.reshape(h.shape), from_rows(moved, p.shape), from_rows(force, p.shape)

    h, p, _ = step(particle_descriptors[0], particle_locations_all[0], earlier_jitter[0])
    beads = h.shape[2]
    piece = beads // replicas

    def trade(values, flat):
        spread = lax.all_to_all(values.reshape(flat), "rep", split_axis=1, concat_axis=1, tiled=True)
        routed = lax.all_to_all(
            jnp.take(spread, partner_choice, axis=1), "rep", split_axis=1, concat_axis=1, tiled=True
        )
        return routed.reshape(values.shape)

    h = trade(h, (tx * ty, replicas, piece * feats))
    p = trade(p, (3 * tx * ty, replicas, piece))
    h, p, force = step(h, p, later_jitter[0])
    return h[None], p[None], force[None]


def solution(mesh):
    in_specs = (
        P("rep", "gx", "gy", None, None),
        P("rep", None, "gx", "gy", None),
        P("rep", None, "gx", "gy", None),
        P("rep", None, "gx", "gy", None),
        P("gx", "gy", None),
        P(),
        P("rep"),
        P(),
        P(),
        P(),
        P(),
        P(),
        P(),
        P(),
    )
    out_specs = (
        P("rep", "gx", "gy", None, None),
        P("rep", None, "gx", "gy", None),
        P("rep", None, "gx", "gy", None),
    )
    return jax.shard_map(
        per_device, mesh=mesh, in_specs=in_specs, out_specs=out_specs, check_vma=False
    )
```

time: 153 us -> 119 us (0.78)
  matrix products: 21.8 us -> 0 us
  other arithmetic: 23.2 us -> 2.67 us
  Pallas kernels: 0 us -> 20.5 us
  local copies, waits for them, and re-layouts: 24.8 us -> 10.1 us
  starting transfers between devices: 50.3 us -> 59.3 us
  waiting for transfers between devices: 28.6 us -> 23.2 us
    dot_general x22 -> x0, matrix products: 21.8 us -> none  [the longest x8 15.6 us: tile_terms(): jnp.einsum('ihd,njhd->hinj', queries, keys_heads, preferred_element_type=...]
    pallas_call x0 -> x2, Pallas kernels: none -> 20.5 us  [run_step(): pl.pallas_call(functools.partial(step_kernel, dims), out_shape=(jax.Shape...]
    gather x34 -> x2, local copies, waits for them, and re-layouts: 14.9 us -> 1.22 us  [trade(): jnp.take(spread, partner_choice, axis=1)]
    mul x18 -> x0, other arithmetic: 11.6 us -> none  [the longest x8 11.3 us: tile_terms(): envelope = envelope * occupied_flags.astype(jnp.float32)[None, :, None]]
    all_to_all x4, waiting for transfers between devices: 22.9 us -> 16 us  [the longest x2 8.6 us: trade(): lax.all_to_all(jnp.take(spread, partner_choice, axis=1), 'rep', split_axi...]
    reduce_sum x21 -> x0, other arithmetic: 6.81 us -> none  [the longest x8 2.2 us: tile_terms(): jnp.sum(offsets * (mixing * probe_values[None, :, :])[None], axis=(2, 3))]
    ppermute x8, starting transfers between devices: 23.9 us -> 30.3 us  [with_halo(): lax.ppermute(tail, axis, [(i, (i + 1) % count) for i in range(ends)])]
    slice x30 -> x2, local copies, waits for them, and re-layouts: 3.97 us -> 0.01 us  [from_rows(): return rows[:, :3].transpose(1, 0, 2).reshape(shape)]
  transfers between devices with their start and end apart: 20 -> 20, of which waited for: 8 -> 9; matrix products, arithmetic and copies ran while one was open for 5% -> 4% of each run, Pallas kernels for 0% -> 0%
where the time goes in v1:
time: 119 us; the launch traced here: 118 us
  starting transfers between devices  59.3 us (50%)
  waiting for transfers between devices  23.2 us (19%)
  Pallas kernels  20.5 us (17%)
  local copies, waits for them, and re-layouts  10.1 us (8%)
  other arithmetic  2.67 us (2%)
  between operations  1.87 us (2%)
    ppermute x8, starting transfers between devices, with_halo(): lax.ppermute(tail, axis, [(i, (i + 1) % count) for i in range(ends)])  30.3 us
    pallas_call x2, Pallas kernels, run_step(): pl.pallas_call(functools.partial(step_kernel, dims), out_shape=(jax.Shape...  20.5 us
    all_to_all x2, starting transfers between devices, trade(): lax.all_to_all(values.reshape(flat), 'rep', split_axis=1, concat_axis=1,...  10.4 us
    ppermute x8, starting transfers between devices, with_halo(): lax.ppermute(head, axis, [((i + 1) % count, i) for i in range(ends)])  10.3 us
    all_to_all x2, waiting for transfers between devices, trade(): lax.all_to_all(jnp.take(spread, partner_choice, axis=1), 'rep', split_axi...  8.6 us
    all_to_all x2, starting transfers between devices, trade(): lax.all_to_all(jnp.take(spread, partner_choice, axis=1), 'rep', split_axi...  8.36 us
    all_to_all x2, waiting for transfers between devices, trade(): lax.all_to_all(values.reshape(flat), 'rep', split_axis=1, concat_axis=1,...  7.38 us
    unnamed x38, local copies, waits for them, and re-layouts  5.15 us
  transfers between devices with their start and end apart: 20, of which 9 were waited for; matrix products, arithmetic and copies ran while one was open for 4% of the time, Pallas kernels for 0%

profile of v1, /device:TPU:0, one launch (start us, length us, event | category | flops | bytes accessed | tf_op | source)
XLA Modules:
  0.0 117.7 jit_solution(4035676040439118152)
XLA Ops:
  0.6 0.9 slice_bitcast_fusion.1
  1.5 1.3 %collective-permute-start.1 = (bf16[1,2,128,128]{3,2,1,0:T(8,128)(2,1)S(1)}, bf16[1,2,128,128]{3,2,1,0:T(8,128)(2,1)S(1)}, u32[]{:S(2)}, u32[]{:S(2)}) collective-permute-start(bf16[1,2,128,128]{3,2,1,0:T(8,128)(2,1)S(1)} %get-tuple-element.29), channel_id=1, source_target_pairs={{2,0},{3,1},{6,4},{7,5},{10,8},{11,9},{14,12},{15,13},{18,16},{19,... | collective-permute-start | bytes 196616 | tf_op jit(solution)/shard_map/ppermute | solution.py:179
  2.8 4.8 %collective-permute-start = (bf16[1,2,128,128]{3,2,1,0:T(8,128)(2,1)S(1)}, bf16[1,2,128,128]{3,2,1,0:T(8,128)(2,1)S(1)}, u32[]{:S(2)}, u32[]{:S(2)}) collective-permute-start(bf16[1,2,128,128]{3,2,1,0:T(8,128)(2,1)S(1)} %get-tuple-element.28), channel_id=1, source_target_pairs={{0,2},{1,3},{4,6},{5,7},{8,10},{9,11},{12,14},{13,15},{16,18},{17,... | collective-permute-start | bytes 196616 | tf_op jit(solution)/shard_map/ppermute | solution.py:177
  7.7 1.3 %collective-permute-start.5 = (f32[3,1,2,128]{3,2,1,0:T(2,128)S(1)}, f32[3,1,2,128]{3,2,1,0:T(2,128)S(1)}, u32[]{:S(2)}, u32[]{:S(2)}) collective-permute-start(f32[3,1,2,128]{3,2,1,0:T(2,128)S(1)} %get-tuple-element.37), channel_id=1, source_target_pairs={{2,0},{3,1},{6,4},{7,5},{10,8},{11,9},{14,12},{15,13},{18,16},{19,... | collective-permute-start | bytes 9224 | tf_op jit(solution)/shard_map/ppermute | solution.py:179
  9.0 4.5 %collective-permute-start.4 = (f32[3,1,2,128]{3,2,1,0:T(2,128)S(1)}, f32[3,1,2,128]{3,2,1,0:T(2,128)S(1)}, u32[]{:S(2)}, u32[]{:S(2)}) collective-permute-start(f32[3,1,2,128]{3,2,1,0:T(2,128)S(1)} %get-tuple-element.36), channel_id=1, source_target_pairs={{0,2},{1,3},{4,6},{5,7},{8,10},{9,11},{12,14},{13,15},{16,18},{17,... | collective-permute-start | bytes 9224 | tf_op jit(solution)/shard_map/ppermute | solution.py:177
  13.8 0.4 copy-done.11
  14.3 0.6 collective-permute-done.4
  14.9 1.3 %collective-permute-start.7 = (f32[3,4,1,128]{3,2,1,0:T(1,128)S(1)}, f32[3,4,1,128]{3,2,1,0:T(1,128)S(1)}, u32[]{:S(2)}, u32[]{:S(2)}) collective-permute-start(f32[3,4,1,128]{3,2,1,0:T(1,128)S(1)} %get-tuple-element.33), channel_id=1, source_target_pairs={{1,0},{3,2},{5,4},{7,6},{9,8},{11,10},{13,12},{15,14},{17,16},{19,... | collective-permute-start | bytes 18440 | tf_op jit(solution)/shard_map/ppermute | solution.py:179
  16.2 3.0 %collective-permute-start.6 = (f32[3,4,1,128]{3,2,1,0:T(1,128)S(1)}, f32[3,4,1,128]{3,2,1,0:T(1,128)S(1)}, u32[]{:S(2)}, u32[]{:S(2)}) collective-permute-start(f32[3,4,1,128]{3,2,1,0:T(1,128)S(1)} %get-tuple-element.32), channel_id=1, source_target_pairs={{0,1},{2,3},{4,5},{6,7},{8,9},{10,11},{12,13},{14,15},{16,17},{18,... | collective-permute-start | bytes 18440 | tf_op jit(solution)/shard_map/ppermute | solution.py:177
  20.1 0.6 copy-done.12
  20.7 0.6 dynamic_slice.3
  21.5 1.3 %collective-permute-start.3 = (bf16[4,1,128,128]{3,2,1,0:T(8,128)(2,1)S(1)}, bf16[4,1,128,128]{3,2,1,0:T(8,128)(2,1)S(1)}, u32[]{:S(2)}, u32[]{:S(2)}) collective-permute-start(bf16[4,1,128,128]{3,2,1,0:T(8,128)(2,1)S(1)} %get-tuple-element.25), channel_id=1, source_target_pairs={{1,0},{3,2},{5,4},{7,6},{9,8},{11,10},{13,12},{15,14},{17,16},{19,... | collective-permute-start | bytes 393224 | tf_op jit(solution)/shard_map/ppermute | solution.py:179
  22.8 3.0 %collective-permute-start.2 = (bf16[4,1,128,128]{3,2,1,0:T(8,128)(2,1)S(1)}, bf16[4,1,128,128]{3,2,1,0:T(8,128)(2,1)S(1)}, u32[]{:S(2)}, u32[]{:S(2)}) collective-permute-start(bf16[4,1,128,128]{3,2,1,0:T(8,128)(2,1)S(1)} %get-tuple-element.24), channel_id=1, source_target_pairs={{0,1},{2,3},{4,5},{6,7},{8,9},{10,11},{12,13},{14,15},{16,17},{18,... | collective-permute-start | bytes 393224 | tf_op jit(solution)/shard_map/ppermute | solution.py:177
  25.9 0.9 collective-permute-done.2
  26.9 0.6 copy-done.10
  27.5 0.5 copy-done.3
  28.1 10.2 %shard_map.157 = (bf16[4,128,128]{2,1,0:T(8,128)(2,1)S(1)}, f32[4,8,128]{2,1,0:T(8,128)S(1)}, f32[4,8,128]{2,1,0:T(8,128)}) custom-call(bf16[16,128,128]{2,1,0:T(8,128)(2,1)S(1)} %bitcast.52, f32[16,8,128]{2,1,0:T(8,128)S(1)} %maximum_maximum_fusion.pos_ref, f32[4,8,128]{2,1,0:T(8,128)S(1)} %get-tuple-element.39.noise_ref, s32[4,6]{1,0:T(4,128)S(1)} %bitcast.53, ...), custom_call_target="tpu_custom_call" | custom-call | tf_op jit(solution)/shard_map/pallas_call | solution.py:150
  38.4 0.7 reshape.68
  39.1 7.0 %all-to-all-start.2 = ((f32[8,1,192]{2,1,0:T(1,128)}), f32[8,1,192]{2,1,0:T(1,128)S(1)}, u32[]{:S(2)}, u32[]{:S(2)}) async-start(f32[8,1,192]{2,1,0:T(1,128)} %reshape.68), calls=%async_computation.2 | async-start | bytes 16384 | tf_op jit(solution)/shard_map/all_to_all | solution.py:239
  46.1 6.5 %all-to-all-done.2 = f32[8,1,192]{2,1,0:T(1,128)S(1)} async-done(((f32[8,1,192]{2,1,0:T(1,128)}), f32[8,1,192]{2,1,0:T(1,128)S(1)}, u32[]{:S(2)}, u32[]{:S(2)}) %all-to-all-start.2) | async-done | bytes 6176 | tf_op jit(solution)/shard_map/all_to_all | solution.py:239
  52.6 0.5 broadcast.72
  53.2 0.7 reduce
  53.9 0.6 gather_fusion.1
  54.5 0.7 reshape.70
  55.3 3.3 %all-to-all-start.3 = ((f32[8,1,192]{2,1,0:T(1,128)}), f32[8,1,192]{2,1,0:T(1,128)S(1)}, u32[]{:S(2)}, u32[]{:S(2)}) async-start(f32[8,1,192]{2,1,0:T(1,128)} %reshape.70), calls=%async_computation.3 | async-start | bytes 16384 | tf_op jit(solution)/shard_map/all_to_all | solution.py:240
  58.6 0.8 copy.34
  59.4 5.6 %all-to-all-done.3 = f32[8,1,192]{2,1,0:T(1,128)S(1)} async-done(((f32[8,1,192]{2,1,0:T(1,128)}), f32[8,1,192]{2,1,0:T(1,128)S(1)}, u32[]{:S(2)}, u32[]{:S(2)}) %all-to-all-start.3) | async-done | bytes 6176 | tf_op jit(solution)/shard_map/all_to_all | solution.py:240
  65.0 3.4 %all-to-all-start = ((bf16[4,8,2048]{2,0,1:T(4,128)(2,1)}), bf16[4,8,2048]{2,0,1:T(4,128)(2,1)S(1)}, u32[]{:S(2)}, u32[]{:S(2)}) async-start(bf16[4,8,2048]{2,0,1:T(4,128)(2,1)} %copy.34), calls=%async_computation | async-start | bytes 262144 | tf_op jit(solution)/shard_map/all_to_all | solution.py:239
  68.4 0.7 reduce.1
  69.3 4.2 %collective-permute-start.12 = (f32[3,1,2,128]{3,2,1,0:T(2,128)S(1)}, f32[3,1,2,128]{3,2,1,0:T(2,128)S(1)}, u32[]{:S(2)}, u32[]{:S(2)}) collective-permute-start(f32[3,1,2,128]{3,2,1,0:T(2,128)S(1)} %get-tuple-element.35), channel_id=1, source_target_pairs={{0,2},{1,3},{4,6},{5,7},{8,10},{9,11},{12,14},{13,15},{16,18},{17,... | collective-permute-start | bytes 9224 | tf_op jit(solution)/shard_map/ppermute | solution.py:177
  73.5 1.3 %collective-permute-start.13 = (f32[3,1,2,128]{3,2,1,0:T(2,128)S(1)}, f32[3,1,2,128]{3,2,1,0:T(2,128)S(1)}, u32[]{:S(2)}, u32[]{:S(2)}) collective-permute-start(f32[3,1,2,128]{3,2,1,0:T(2,128)S(1)} %get-tuple-element.34), channel_id=1, source_target_pairs={{2,0},{3,1},{6,4},{7,5},{10,8},{11,9},{14,12},{15,13},{18,16},{19,... | collective-permute-start | bytes 9224 | tf_op jit(solution)/shard_map/ppermute | solution.py:179
  74.8 0.9 all-to-all-done
  75.7 0.7 gather_fusion
  76.3 0.8 select_bitcast_fusion
  77.1 5.1 %all-to-all-start.1 = ((bf16[4,8,2048]{2,0,1:T(4,128)(2,1)}), bf16[4,8,2048]{2,0,1:T(4,128)(2,1)S(1)}, u32[]{:S(2)}, u32[]{:S(2)}) async-start(bf16[4,8,2048]{2,0,1:T(4,128)(2,1)} %select_bitcast_fusion), calls=%async_computation.1 | async-start | bytes 262144 | tf_op jit(solution)/shard_map/all_to_all | solution.py:240
  82.2 1.3 %collective-permute-start.15 = (f32[3,4,1,128]{3,2,1,0:T(1,128)S(1)}, f32[3,4,1,128]{3,2,1,0:T(1,128)S(1)}, u32[]{:S(2)}, u32[]{:S(2)}) collective-permute-start(f32[3,4,1,128]{3,2,1,0:T(1,128)S(1)} %get-tuple-element.31), channel_id=1, source_target_pairs={{1,0},{3,2},{5,4},{7,6},{9,8},{11,10},{13,12},{15,14},{17,16},{19,... | collective-permute-start | bytes 18440 | tf_op jit(solution)/shard_map/ppermute | solution.py:179
  83.5 3.0 %collective-permute-start.14 = (f32[3,4,1,128]{3,2,1,0:T(1,128)S(1)}, f32[3,4,1,128]{3,2,1,0:T(1,128)S(1)}, u32[]{:S(2)}, u32[]{:S(2)}) collective-permute-start(f32[3,4,1,128]{3,2,1,0:T(1,128)S(1)} %get-tuple-element.30), channel_id=1, source_target_pairs={{0,1},{2,3},{4,5},{6,7},{8,9},{10,11},{12,13},{14,15},{16,17},{18,... | collective-permute-start | bytes 18440 | tf_op jit(solution)/shard_map/ppermute | solution.py:177
  86.6 3.0 %all-to-all-done.1 = bf16[4,8,2048]{2,0,1:T(4,128)(2,1)S(1)} async-done(((bf16[4,8,2048]{2,0,1:T(4,128)(2,1)}), bf16[4,8,2048]{2,0,1:T(4,128)(2,1)S(1)}, u32[]{:S(2)}, u32[]{:S(2)}) %all-to-all-start.1) | async-done | bytes 131104 | tf_op jit(solution)/shard_map/all_to_all | solution.py:240
  89.7 4.5 %collective-permute-start.8 = (bf16[1,2,128,128]{3,2,1,0:T(8,128)(2,1)S(1)}, bf16[1,2,128,128]{3,2,1,0:T(8,128)(2,1)S(1)}, u32[]{:S(2)}, u32[]{:S(2)}) collective-permute-start(bf16[1,2,128,128]{3,2,1,0:T(8,128)(2,1)S(1)} %slice.80), channel_id=1, source_target_pairs={{0,2},{1,3},{4,6},{5,7},{8,10},{9,11},{12,14},{13,15},{16,18},{17,... | collective-permute-start | bytes 196616 | tf_op jit(solution)/shard_map/ppermute | solution.py:177
  94.6 1.3 %collective-permute-start.9 = (bf16[1,2,128,128]{3,2,1,0:T(8,128)(2,1)S(1)}, bf16[1,2,128,128]{3,2,1,0:T(8,128)(2,1)S(1)}, u32[]{:S(2)}, u32[]{:S(2)}) collective-permute-start(bf16[1,2,128,128]{3,2,1,0:T(8,128)(2,1)S(1)} %slice.82), channel_id=1, source_target_pairs={{2,0},{3,1},{6,4},{7,5},{10,8},{11,9},{14,12},{15,13},{18,16},{19,... | collective-permute-start | bytes 196616 | tf_op jit(solution)/shard_map/ppermute | solution.py:179
  95.9 0.3 collective-permute-done.8
  96.2 4.6 %collective-permute-done.9 = bf16[1,2,128,128]{3,2,1,0:T(8,128)(2,1)S(1)} collective-permute-done((bf16[1,2,128,128]{3,2,1,0:T(8,128)(2,1)S(1)}, bf16[1,2,128,128]{3,2,1,0:T(8,128)(2,1)S(1)}, u32[]{:S(2)}, u32[]{:S(2)}) %collective-permute-start.9) | collective-permute-done | bytes 65568 | tf_op jit(solution)/shard_map/ppermute | solution.py:179
  100.8 1.3 %collective-permute-start.11 = (bf16[4,1,128,128]{3,2,1,0:T(8,128)(2,1)S(1)}, bf16[4,1,128,128]{3,2,1,0:T(8,128)(2,1)S(1)}, u32[]{:S(2)}, u32[]{:S(2)}) collective-permute-start(bf16[4,1,128,128]{3,2,1,0:T(8,128)(2,1)S(1)} %get-tuple-element.23), channel_id=1, source_target_pairs={{1,0},{3,2},{5,4},{7,6},{9,8},{11,10},{13,12},{15,14},{17,16},{19,... | collective-permute-start | bytes 393224 | tf_op jit(solution)/shard_map/ppermute | solution.py:179
  102.1 3.0 %collective-permute-start.10 = (bf16[4,1,128,128]{3,2,1,0:T(8,128)(2,1)S(1)}, bf16[4,1,128,128]{3,2,1,0:T(8,128)(2,1)S(1)}, u32[]{:S(2)}, u32[]{:S(2)}) collective-permute-start(bf16[4,1,128,128]{3,2,1,0:T(8,128)(2,1)S(1)} %get-tuple-element.22), channel_id=1, source_target_pairs={{0,1},{2,3},{4,5},{6,7},{8,9},{10,11},{12,13},{14,15},{16,17},{18,... | collective-permute-start | bytes 393224 | tf_op jit(solution)/shard_map/ppermute | solution.py:177
  105.2 0.9 collective-permute-done.10
  106.1 10.3 %shard_map.158 = (bf16[4,128,128]{2,1,0:T(8,128)(2,1)}, f32[4,8,128]{2,1,0:T(8,128)S(1)}, f32[4,8,128]{2,1,0:T(8,128)S(1)}) custom-call(bf16[16,128,128]{2,1,0:T(8,128)(2,1)S(1)} %bitcast.51, f32[16,8,128]{2,1,0:T(8,128)S(1)} %maximum_maximum_fusion.1.pos_ref, f32[4,8,128]{2,1,0:T(8,128)S(1)} %get-tuple-element.38.noise_ref, s32[4,6]{1,0:T(4,128)S(1)} %bitcast.54, ...), custom_call_target="tpu_custom_call" | custom-call | tf_op jit(solution)/shard_map/pallas_call | solution.py:150
  116.5 0.6 copy.43
  117.1 0.6 copy.44
  (86 shorter events, 1.9 us)
Async XLA Ops:
  0.6 7.1 %copy-start.7 = (f32[1,3,2,2,128]{4,3,2,1,0:T(2,128)S(1)}, f32[1,3,2,2,128]{4,3,2,1,0:T(2,128)}, u32[]{:S(2)}) copy-start(f32[1,3,2,2,128]{4,3,2,1,0:T(2,128)} %param.15) | copy-start | bytes 18436
  1.5 19.8 %collective-permute-start.1 = (bf16[1,2,128,128]{3,2,1,0:T(8,128)(2,1)S(1)}, bf16[1,2,128,128]{3,2,1,0:T(8,128)(2,1)S(1)}, u32[]{:S(2)}, u32[]{:S(2)}) collective-permute-start(bf16[1,2,128,128]{3,2,1,0:T(8,128)(2,1)S(1)} %get-tuple-element.29), channel_id=1, source_target_pairs={{2,0},{3,1},{6,4},{7,5},{10,8},{11,9},{14,12},{15,13},{18,16},{19,... | collective-permute-start | bytes 196616 | tf_op jit(solution)/shard_map/ppermute | solution.py:179
  2.8 18.5 %collective-permute-start = (bf16[1,2,128,128]{3,2,1,0:T(8,128)(2,1)S(1)}, bf16[1,2,128,128]{3,2,1,0:T(8,128)(2,1)S(1)}, u32[]{:S(2)}, u32[]{:S(2)}) collective-permute-start(bf16[1,2,128,128]{3,2,1,0:T(8,128)(2,1)S(1)} %get-tuple-element.28), channel_id=1, source_target_pairs={{0,2},{1,3},{4,6},{5,7},{8,10},{9,11},{12,14},{13,15},{16,18},{17,... | collective-permute-start | bytes 196616 | tf_op jit(solution)/shard_map/ppermute | solution.py:177
  7.7 5.9 %copy-start.8 = (f32[1,3,2,2,128]{4,3,2,1,0:T(2,128)S(1)}, f32[1,3,2,2,128]{4,3,2,1,0:T(2,128)}, u32[]{:S(2)}) copy-start(f32[1,3,2,2,128]{4,3,2,1,0:T(2,128)} %param.17) | copy-start | bytes 18436
  7.7 6.5 %collective-permute-start.5 = (f32[3,1,2,128]{3,2,1,0:T(2,128)S(1)}, f32[3,1,2,128]{3,2,1,0:T(2,128)S(1)}, u32[]{:S(2)}, u32[]{:S(2)}) collective-permute-start(f32[3,1,2,128]{3,2,1,0:T(2,128)S(1)} %get-tuple-element.37), channel_id=1, source_target_pairs={{2,0},{3,1},{6,4},{7,5},{10,8},{11,9},{14,12},{15,13},{18,16},{19,... | collective-permute-start | bytes 9224 | tf_op jit(solution)/shard_map/ppermute | solution.py:179
  9.0 4.6 %copy-start.9 = (f32[1,3,2,2,128]{4,3,2,1,0:T(2,128)S(1)}, f32[1,3,2,2,128]{4,3,2,1,0:T(2,128)}, u32[]{:S(2)}) copy-start(f32[1,3,2,2,128]{4,3,2,1,0:T(2,128)} %param.16) | copy-start | bytes 18436
  9.0 5.9 %collective-permute-start.4 = (f32[3,1,2,128]{3,2,1,0:T(2,128)S(1)}, f32[3,1,2,128]{3,2,1,0:T(2,128)S(1)}, u32[]{:S(2)}, u32[]{:S(2)}) collective-permute-start(f32[3,1,2,128]{3,2,1,0:T(2,128)S(1)} %get-tuple-element.36), channel_id=1, source_target_pairs={{0,2},{1,3},{4,6},{5,7},{8,10},{9,11},{12,14},{13,15},{16,18},{17,... | collective-permute-start | bytes 9224 | tf_op jit(solution)/shard_map/ppermute | solution.py:177
  13.6 0.7 copy-start.11
  13.6 7.8 %copy-start.6 = (bf16[1,2,2,128,128]{4,3,2,1,0:T(8,128)(2,1)S(1)}, bf16[1,2,2,128,128]{4,3,2,1,0:T(8,128)(2,1)}, u32[]{:S(2)}) copy-start(bf16[1,2,2,128,128]{4,3,2,1,0:T(8,128)(2,1)} %param.14) | copy-start | bytes 393220
  14.9 6.4 %collective-permute-start.7 = (f32[3,4,1,128]{3,2,1,0:T(1,128)S(1)}, f32[3,4,1,128]{3,2,1,0:T(1,128)S(1)}, u32[]{:S(2)}, u32[]{:S(2)}) collective-permute-start(f32[3,4,1,128]{3,2,1,0:T(1,128)S(1)} %get-tuple-element.33), channel_id=1, source_target_pairs={{1,0},{3,2},{5,4},{7,6},{9,8},{11,10},{13,12},{15,14},{17,16},{19,... | collective-permute-start | bytes 18440 | tf_op jit(solution)/shard_map/ppermute | solution.py:179
  16.2 5.1 %collective-permute-start.6 = (f32[3,4,1,128]{3,2,1,0:T(1,128)S(1)}, f32[3,4,1,128]{3,2,1,0:T(1,128)S(1)}, u32[]{:S(2)}, u32[]{:S(2)}) collective-permute-start(f32[3,4,1,128]{3,2,1,0:T(1,128)S(1)} %get-tuple-element.32), channel_id=1, source_target_pairs={{0,1},{2,3},{4,5},{6,7},{8,9},{10,11},{12,13},{14,15},{16,17},{18,... | collective-permute-start | bytes 18440 | tf_op jit(solution)/shard_map/ppermute | solution.py:177
  20.1 0.7 copy-start.12
  21.5 4.4 %collective-permute-start.3 = (bf16[4,1,128,128]{3,2,1,0:T(8,128)(2,1)S(1)}, bf16[4,1,128,128]{3,2,1,0:T(8,128)(2,1)S(1)}, u32[]{:S(2)}, u32[]{:S(2)}) collective-permute-start(bf16[4,1,128,128]{3,2,1,0:T(8,128)(2,1)S(1)} %get-tuple-element.25), channel_id=1, source_target_pairs={{1,0},{3,2},{5,4},{7,6},{9,8},{11,10},{13,12},{15,14},{17,16},{19,... | collective-permute-start | bytes 393224 | tf_op jit(solution)/shard_map/ppermute | solution.py:179
  22.8 4.0 %collective-permute-start.2 = (bf16[4,1,128,128]{3,2,1,0:T(8,128)(2,1)S(1)}, bf16[4,1,128,128]{3,2,1,0:T(8,128)(2,1)S(1)}, u32[]{:S(2)}, u32[]{:S(2)}) collective-permute-start(bf16[4,1,128,128]{3,2,1,0:T(8,128)(2,1)S(1)} %get-tuple-element.24), channel_id=1, source_target_pairs={{0,1},{2,3},{4,5},{6,7},{8,9},{10,11},{12,13},{14,15},{16,17},{18,... | collective-permute-start | bytes 393224 | tf_op jit(solution)/shard_map/ppermute | solution.py:177
  25.9 1.5 %copy-start = (bf16[128,384]{1,0:T(8,128)(2,1)S(1)}, bf16[128,384]{1,0:T(8,128)(2,1)}, u32[]{:S(2)}) copy-start(bf16[128,384]{1,0:T(8,128)(2,1)} %weight.3) | copy-start | bytes 294916
  26.8 0.7 copy-start.10
  26.8 0.8 copy-start.1
  26.8 0.7 copy-start.2
  27.4 0.7 copy-start.3
  27.4 0.7 copy-start.4
  27.4 0.7 copy-start.5
  39.1 13.5 %all-to-all-start.2 = ((f32[8,1,192]{2,1,0:T(1,128)}), f32[8,1,192]{2,1,0:T(1,128)S(1)}, u32[]{:S(2)}, u32[]{:S(2)}) async-start(f32[8,1,192]{2,1,0:T(1,128)} %reshape.68), calls=%async_computation.2 | async-start | bytes 16384 | tf_op jit(solution)/shard_map/all_to_all | solution.py:239
  55.3 9.7 %all-to-all-start.3 = ((f32[8,1,192]{2,1,0:T(1,128)}), f32[8,1,192]{2,1,0:T(1,128)S(1)}, u32[]{:S(2)}, u32[]{:S(2)}) async-start(f32[8,1,192]{2,1,0:T(1,128)} %reshape.70), calls=%async_computation.3 | async-start | bytes 16384 | tf_op jit(solution)/shard_map/all_to_all | solution.py:240
  65.0 10.7 %all-to-all-start = ((bf16[4,8,2048]{2,0,1:T(4,128)(2,1)}), bf16[4,8,2048]{2,0,1:T(4,128)(2,1)S(1)}, u32[]{:S(2)}, u32[]{:S(2)}) async-start(bf16[4,8,2048]{2,0,1:T(4,128)(2,1)} %copy.34), calls=%async_computation | async-start | bytes 262144 | tf_op jit(solution)/shard_map/all_to_all | solution.py:239
  69.3 5.5 %collective-permute-start.12 = (f32[3,1,2,128]{3,2,1,0:T(2,128)S(1)}, f32[3,1,2,128]{3,2,1,0:T(2,128)S(1)}, u32[]{:S(2)}, u32[]{:S(2)}) collective-permute-start(f32[3,1,2,128]{3,2,1,0:T(2,128)S(1)} %get-tuple-element.35), channel_id=1, source_target_pairs={{0,2},{1,3},{4,6},{5,7},{8,10},{9,11},{12,14},{13,15},{16,18},{17,... | collective-permute-start | bytes 9224 | tf_op jit(solution)/shard_map/ppermute | solution.py:177
  73.5 8.7 %collective-permute-start.13 = (f32[3,1,2,128]{3,2,1,0:T(2,128)S(1)}, f32[3,1,2,128]{3,2,1,0:T(2,128)S(1)}, u32[]{:S(2)}, u32[]{:S(2)}) collective-permute-start(f32[3,1,2,128]{3,2,1,0:T(2,128)S(1)} %get-tuple-element.34), channel_id=1, source_target_pairs={{2,0},{3,1},{6,4},{7,5},{10,8},{11,9},{14,12},{15,13},{18,16},{19,... | collective-permute-start | bytes 9224 | tf_op jit(solution)/shard_map/ppermute | solution.py:179
  77.1 12.4 %all-to-all-start.1 = ((bf16[4,8,2048]{2,0,1:T(4,128)(2,1)}), bf16[4,8,2048]{2,0,1:T(4,128)(2,1)S(1)}, u32[]{:S(2)}, u32[]{:S(2)}) async-start(bf16[4,8,2048]{2,0,1:T(4,128)(2,1)} %select_bitcast_fusion), calls=%async_computation.1 | async-start | bytes 262144 | tf_op jit(solution)/shard_map/all_to_all | solution.py:240
  82.2 12.0 %collective-permute-start.15 = (f32[3,4,1,128]{3,2,1,0:T(1,128)S(1)}, f32[3,4,1,128]{3,2,1,0:T(1,128)S(1)}, u32[]{:S(2)}, u32[]{:S(2)}) collective-permute-start(f32[3,4,1,128]{3,2,1,0:T(1,128)S(1)} %get-tuple-element.31), channel_id=1, source_target_pairs={{1,0},{3,2},{5,4},{7,6},{9,8},{11,10},{13,12},{15,14},{17,16},{19,... | collective-permute-start | bytes 18440 | tf_op jit(solution)/shard_map/ppermute | solution.py:179
  83.5 10.7 %collective-permute-start.14 = (f32[3,4,1,128]{3,2,1,0:T(1,128)S(1)}, f32[3,4,1,128]{3,2,1,0:T(1,128)S(1)}, u32[]{:S(2)}, u32[]{:S(2)}) collective-permute-start(f32[3,4,1,128]{3,2,1,0:T(1,128)S(1)} %get-tuple-element.30), channel_id=1, source_target_pairs={{0,1},{2,3},{4,5},{6,7},{8,9},{10,11},{12,13},{14,15},{16,17},{18,... | collective-permute-start | bytes 18440 | tf_op jit(solution)/shard_map/ppermute | solution.py:177
  89.7 6.4 %collective-permute-start.8 = (bf16[1,2,128,128]{3,2,1,0:T(8,128)(2,1)S(1)}, bf16[1,2,128,128]{3,2,1,0:T(8,128)(2,1)S(1)}, u32[]{:S(2)}, u32[]{:S(2)}) collective-permute-start(bf16[1,2,128,128]{3,2,1,0:T(8,128)(2,1)S(1)} %slice.80), channel_id=1, source_target_pairs={{0,2},{1,3},{4,6},{5,7},{8,10},{9,11},{12,14},{13,15},{16,18},{17,... | collective-permute-start | bytes 196616 | tf_op jit(solution)/shard_map/ppermute | solution.py:177
  94.6 6.2 %collective-permute-start.9 = (bf16[1,2,128,128]{3,2,1,0:T(8,128)(2,1)S(1)}, bf16[1,2,128,128]{3,2,1,0:T(8,128)(2,1)S(1)}, u32[]{:S(2)}, u32[]{:S(2)}) collective-permute-start(bf16[1,2,128,128]{3,2,1,0:T(8,128)(2,1)S(1)} %slice.82), channel_id=1, source_target_pairs={{2,0},{3,1},{6,4},{7,5},{10,8},{11,9},{14,12},{15,13},{18,16},{19,... | collective-permute-start | bytes 196616 | tf_op jit(solution)/shard_map/ppermute | solution.py:179
  100.8 4.4 %collective-permute-start.11 = (bf16[4,1,128,128]{3,2,1,0:T(8,128)(2,1)S(1)}, bf16[4,1,128,128]{3,2,1,0:T(8,128)(2,1)S(1)}, u32[]{:S(2)}, u32[]{:S(2)}) collective-permute-start(bf16[4,1,128,128]{3,2,1,0:T(8,128)(2,1)S(1)} %get-tuple-element.23), channel_id=1, source_target_pairs={{1,0},{3,2},{5,4},{7,6},{9,8},{11,10},{13,12},{15,14},{17,16},{19,... | collective-permute-start | bytes 393224 | tf_op jit(solution)/shard_map/ppermute | solution.py:179
  102.1 4.0 %collective-permute-start.10 = (bf16[4,1,128,128]{3,2,1,0:T(8,128)(2,1)S(1)}, bf16[4,1,128,128]{3,2,1,0:T(8,128)(2,1)S(1)}, u32[]{:S(2)}, u32[]{:S(2)}) collective-permute-start(bf16[4,1,128,128]{3,2,1,0:T(8,128)(2,1)S(1)} %get-tuple-element.22), channel_id=1, source_target_pairs={{0,1},{2,3},{4,5},{6,7},{8,9},{10,11},{12,13},{14,15},{16,17},{18,... | collective-permute-start | bytes 393224 | tf_op jit(solution)/shard_map/ppermute | solution.py:177

commit v2 on v1

v2 whole, which is shorter than its diff:
```python
import functools
import math

import jax
import jax.numpy as jnp
from jax import lax
from jax.experimental import pallas as pl
from jax.experimental.pallas import tpu as pltpu
from jax.sharding import PartitionSpec as P

NORM_EPS = 1e-05
DURATION_DELTA = 0.1
JITTER_SIZE = 0.05
MESSAGE_SCALE = 1.0 / 32.0
FORCE_SCALE = 1.0 / 16.0
LOG2E = math.log2(math.e)


def window_coefficients(degree):
    import numpy as np

    nodes = 0.5 - 0.5 * np.cos(np.pi * (np.arange(64) + 0.5) / 64)
    target = np.cos(0.5 * np.pi * np.sqrt(nodes)) / (1.0 - nodes)
    return [float(c) for c in np.polyfit(nodes, target, degree)]


WINDOW = window_coefficients(4)


def project(h, gain_row, weight):
    values = h.astype(jnp.float32)
    center = jnp.mean(values, axis=-1, keepdims=True)
    centred = values - center
    spread = jnp.mean(centred * centred, axis=-1, keepdims=True)
    normed = (centred * lax.rsqrt(spread + NORM_EPS) * gain_row).astype(jnp.bfloat16)
    return jnp.dot(normed, weight, preferred_element_type=jnp.float32).astype(jnp.bfloat16)


def tall(block):
    rows, lanes = block.shape
    return jnp.concatenate([block, jnp.zeros((lanes - rows, lanes), block.dtype)], axis=0)


def prepare_tile(t, h, pos, gain_row, weight, charge, k_ref, rhs_ref, near_ref):
    feats = h.shape[1]
    proj = project(h, gain_row, weight)
    keys = proj[:, feats : 2 * feats]
    near_ref[t] = pos
    k_ref[t] = keys
    rhs_ref[t, :, :feats] = proj[:, 2 * feats :]
    probe = lax.dot_general(
        charge, keys, (((1,), (1,)), ((), ())), preferred_element_type=jnp.float32
    )
    rows = probe * pos
    high = rows.astype(jnp.bfloat16).astype(jnp.float32)
    columns = tall(jnp.concatenate([high, rows - high], axis=0)).T
    rhs_ref[t, :, feats:] = columns.astype(jnp.bfloat16)
    return proj[:, :feats]


def score_slots(i, group, own, q, pos, slot_of, work, s_ref, falloff):
    k_ref, near_ref = work.k, work.near
    beads, feats = q.shape
    heads = falloff.shape[0]
    lane = lax.broadcasted_iota(jnp.int32, (beads, feats), 1) // (feats // heads)
    zero = jnp.zeros_like(q)
    stacked = jnp.concatenate([jnp.where(lane == e, q, zero) for e in range(heads)], axis=0)
    columns = tall(pos).T
    for part in group:
        where = [jnp.where(slot_of(n) >= 0, slot_of(n), own) for n in part]
        present = [(slot_of(n) >= 0).astype(jnp.float32) for n in part]
        keys = join([k_ref[w] for w in where], 0)
        logits = lax.dot_general(
            stacked, keys, (((1,), (1,)), ((), ())), preferred_element_type=jnp.float32
        )
        near = join([near_ref[w] for w in where], 1)
        occupied = join([jnp.full((1, beads), v, jnp.float32) for v in present], 1)
        squared = None
        for c in range(3):
            offset = columns[:, c : c + 1] - near[c : c + 1, :]
            squared = offset * offset if squared is None else squared + offset * offset
        squared = jnp.minimum(squared, 1.0)
        window = jnp.full_like(squared, WINDOW[0])
        for coefficient in WINDOW[1:]:
            window = window * squared + coefficient
        window = window * (1.0 - squared)
        window = window * window * occupied
        for e in range(heads):
            half = logits[e * beads : (e + 1) * beads]
            act = half + half * jnp.tanh(half)
            score = act * (window * jnp.exp2(squared * (falloff[e] * -LOG2E)))
            s_ref[i, e * beads : (e + 1) * beads, part[0] * beads : (part[-1] + 1) * beads] = (
                score.astype(jnp.bfloat16)
            )


def finish_tile(i, own, h, pos, noise, scale, slot_of, slot_count, work, s_ref, mixing, out_weight):
    beads, feats = h.shape
    heads = mixing.shape[0]
    lane = lax.broadcasted_iota(jnp.int32, (beads, feats), 1) // (feats // heads)
    where = [jnp.where(slot_of(n) >= 0, slot_of(n), own) for n in range(slot_count)]
    rhs = jnp.concatenate([work.rhs[w] for w in where], axis=0)
    sums = jnp.dot(s_ref[i], rhs, preferred_element_type=jnp.float32)
    message = jnp.zeros((beads, feats), jnp.float32)
    pulls = jnp.zeros((beads, feats), jnp.float32)
    for e in range(heads):
        part = sums[e * beads : (e + 1) * beads]
        message = jnp.where(lane == e, part[:, :feats], message)
        pulls = pulls + mixing[e] * part[:, feats:]
    message = (message * MESSAGE_SCALE).astype(jnp.bfloat16)
    mixed = jnp.dot(message, out_weight, preferred_element_type=jnp.float32)
    updated = (h.astype(jnp.float32) + mixed).astype(jnp.bfloat16)
    turned = pulls.T
    turned = turned[0:8] + turned[8:16]
    force = (pos * turned[3:4] - turned) * FORCE_SCALE
    moved = pos + DURATION_DELTA * force + (JITTER_SIZE * scale) * noise
    return updated, moved, force


def join(parts, axis):
    return parts[0] if len(parts) == 1 else jnp.concatenate(parts, axis=axis)


def rows_of(ref, a, b, fill):
    rows = [ref[0, c, a, pl.ds(b, 1), :] for c in range(3)]
    beads = rows[0].shape[1]
    rows.append(jnp.full((1, beads), fill, jnp.float32))
    rows.append(jnp.zeros((4, beads), jnp.float32))
    return jnp.concatenate(rows, axis=0)


class Work:
    def __init__(self, k, rhs, near, q):
        self.k, self.rhs, self.near, self.q = k, rhs, near, q


DIRECTIONS = [(dx, dy) for dx in (-1, 0, 1) for dy in (-1, 0, 1) if (dx, dy) != (0, 0)]


def side(step, size):
    if step == 0:
        return 0, size, 1
    return (size - 1, 1, 0) if step > 0 else (0, 1, size + 1)


def window_kernel(sizes, h_in, p_in, noise1, noise2, slots, levels, heat_slot, partner, gain, weight,
                  out_weight, charge_ref, falloff, mixing, h_out, moved_out, force_out, k_ref,
                  rhs_ref, near_ref, q_ref, s_ref, rim1, rim2, pos1, pos2, mine_h, mine_p, spread_a,
                  spread_b, spread_p, route_h, route_p, trade_h, trade_p, halo_send, halo_recv,
                  swap_send, swap_recv):
    reps, nx, ny = sizes
    _, tx, ty, beads, feats = h_in.shape
    tiles = tx * ty
    ex, ey = tx + 2, ty + 2
    slot_count = slots.shape[2]
    me, gx, gy = lax.axis_index("rep"), lax.axis_index("gx"), lax.axis_index("gy")
    work = Work(k_ref, rhs_ref, near_ref, q_ref)
    scale = jnp.sqrt(jnp.full((1, beads), levels[heat_slot[0]], jnp.float32))
    spread_h = (spread_a, spread_b)
    groups = len(spread_h)
    piece = tiles * beads // groups // reps
    per = mine_p.shape[1]

    def has(dx, dy):
        conds = []
        if dx:
            conds.append(gx < nx - 1 if dx > 0 else gx > 0)
        if dy:
            conds.append(gy < ny - 1 if dy > 0 else gy > 0)
        return conds[0] if len(conds) == 1 else jnp.logical_and(*conds)

    def other(k):
        return (lax.rem(me + k, reps), gx, gy)

    barrier = pltpu.get_barrier_semaphore()
    for k in range(1, reps):
        pl.semaphore_signal(barrier, inc=1, device_id=other(k), device_id_type=pl.DeviceIdType.MESH)
    for dx, dy in DIRECTIONS:
        @pl.when(has(dx, dy))
        def _(dx=dx, dy=dy):
            pl.semaphore_signal(barrier, inc=1, device_id=(me, gx + dx, gy + dy),
                                device_id_type=pl.DeviceIdType.MESH)

    gain_row, weights, out_w = gain[...], weight[...], out_weight[...]
    charge = jnp.broadcast_to(charge_ref[...].astype(jnp.float32), (8, feats)).astype(jnp.bfloat16)

    def prepare(row, col, h, pos):
        q = prepare_tile(row * ey + col, h, pos, gain_row, weights, charge, k_ref, rhs_ref, near_ref)
        if 1 <= row <= tx and 1 <= col <= ty:
            q_ref[(row - 1) * ty + col - 1] = q * jnp.bfloat16(0.125)

    def halo_copies(step, d, h_src, rim, pos):
        dx, dy = DIRECTIONS[d]
        (r0, nr, r1), (c0, nc, c1) = side(dx, tx), side(dy, ty)
        target = (me, gx + dx, gy + dy)
        return [
            pltpu.make_async_remote_copy(
                src_ref=src, dst_ref=dst, send_sem=halo_send.at[step, d, kind],
                recv_sem=halo_recv.at[step, d, kind], device_id=target,
                device_id_type=pl.DeviceIdType.MESH)
            for kind, (src, dst) in enumerate((
                (h_src.at[pl.ds(r0, nr), pl.ds(c0, nc)], rim.at[pl.ds(r1, nr), pl.ds(c1, nc)]),
                (pos.at[pl.ds(r0 + 1, nr), pl.ds(c0 + 1, nc)], pos.at[pl.ds(r1, nr), pl.ds(c1, nc)]),
            ))
        ]

    def slot_reader(i):
        return lambda n: slots[i // ty, lax.rem(i, ty), n]

    def own_of(i):
        return (i // ty + 1) * ey + lax.rem(i, ty) + 1

    def step(number, h_src, rim, pos, noise, finish, after_group):
        for d, (dx, dy) in enumerate(DIRECTIONS):
            @pl.when(has(dx, dy))
            def _(d=d):
                for copy in halo_copies(number, d, h_src, rim, pos):
                    copy.start()

        def self_body(i, carry):
            score_slots(i, ((0,),), own_of(i), q_ref[i], near_ref[own_of(i)], slot_reader(i), work,
                        s_ref, falloff)
            return carry

        lax.fori_loop(0, tiles, self_body, 0)
        for d, (dx, dy) in enumerate(DIRECTIONS):
            @pl.when(has(-dx, -dy))
            def _(d=d, dx=dx, dy=dy):
                for copy in halo_copies(number, d, h_src, rim, pos):
                    copy.wait_recv()
                (_, nr, r1), (_, nc, c1) = side(dx, tx), side(dy, ty)
                for row in range(r1, r1 + nr):
                    for col in range(c1, c1 + nc):
                        prepare(row, col, rim[row, col], pos[row, col])

        rest = [(n, n + 1) if n + 1 < slot_count else (n,) for n in range(1, slot_count, 2)]

        def body(i, carry):
            a, b = i // ty, lax.rem(i, ty)
            here = near_ref[own_of(i)]
            score_slots(i, rest, own_of(i), q_ref[i], here, slot_reader(i), work, s_ref, falloff)
            finish(i, a, b, *finish_tile(
                i, own_of(i), h_src[a, b], here, rows_of(noise, a, b, 0.0), scale, slot_reader(i),
                slot_count, work, s_ref, mixing, out_w))
            return carry

        for g in range(groups):
            lax.fori_loop(g * tiles // groups, (g + 1) * tiles // groups, body, 0)
            after_group(g)
        for d, (dx, dy) in enumerate(DIRECTIONS):
            @pl.when(has(dx, dy))
            def _(d=d):
                for copy in halo_copies(number, d, h_src, rim, pos):
                    copy.wait_send()

    def swap_copy(phase, part, k, src, dst):
        return pltpu.make_async_remote_copy(
            src_ref=src, dst_ref=dst, send_sem=swap_send.at[phase, part, k],
            recv_sem=swap_recv.at[phase, part, k], device_id=other(k),
            device_id_type=pl.DeviceIdType.MESH)

    def first_copy(part, k):
        peer = lax.rem(me + k, reps)
        if part == groups:
            return swap_copy(0, part, k, mine_p.at[peer], spread_p.at[me])
        return swap_copy(0, part, k, mine_h.at[part, peer], spread_h[part].at[me])

    def place(part, owner):
        start = part * (tiles * beads // groups) + owner * piece
        t = start // beads
        return t // ty, lax.rem(t, ty), pl.ds(pl.multiple_of(lax.rem(start, beads), piece), piece)

    def second_copy(part, k):
        if part == groups:
            return swap_copy(1, part, k, route_p.at[k], trade_p.at[me])
        a, b, rows = place(part, me)
        return swap_copy(1, part, k, route_h.at[part, k], trade_h.at[a, b, rows])

    def send_first(part):
        for k in range(1, reps):
            first_copy(part, k).start()
        if part == groups:
            spread_p[me] = mine_p[me]
        else:
            spread_h[part][me] = mine_h[part, me]

    def send_second(part):
        for k in range(1, reps):
            first_copy(part, k).wait_recv()
        for k in range(reps):
            chosen = partner[lax.rem(me + k, reps)]
            if part == groups:
                value = spread_p[chosen]
                if k:
                    route_p[k] = value
                else:
                    trade_p[me] = value
            else:
                value = spread_h[part][chosen]
                if k:
                    route_h[part, k] = value
                else:
                    a, b, rows = place(part, me)
                    trade_h[a, b, rows, :] = value
            if k:
                second_copy(part, k).start()

    def finish_first(i, a, b, updated, moved, force):
        pieces = beads // piece
        for n in range(pieces):
            which = i * pieces + n
            mine_h[which // reps, lax.rem(which, reps)] = updated[n * piece : (n + 1) * piece]
        for c in range(3):
            row = c * tiles + i
            mine_p[row // per, pl.ds(lax.rem(row, per), 1), :] = moved[c : c + 1]

    def after_first(g):
        send_first(g)
        if g:
            send_first(groups)
        if g:
            for part in range(groups + 1):
                send_second(part)

    def finish_second(i, a, b, updated, moved, force):
        h_out[0, a, b] = updated
        for c in range(3):
            moved_out[0, c, a, pl.ds(b, 1), :] = moved[c : c + 1]
            force_out[0, c, a, pl.ds(b, 1), :] = force[c : c + 1]

    for a in range(tx):
        for b in range(ty):
            pos = rows_of(p_in, a, b, 1.0)
            pos1[a + 1, b + 1] = pos
            prepare(a + 1, b + 1, h_in[0, a, b], pos)
    mine_p[...] = jnp.zeros_like(mine_p)

    columns = 1 + jnp.minimum(gx, 1) + jnp.minimum(nx - 1 - gx, 1)
    lines = 1 + jnp.minimum(gy, 1) + jnp.minimum(ny - 1 - gy, 1)
    pl.semaphore_wait(barrier, reps - 2 + columns * lines)

    step(0, h_in.at[0], rim1, pos1, noise1, finish_first, after_first)

    for part in range(groups + 1):
        for k in range(1, reps):
            second_copy(part, k).wait_recv()
    for a in range(tx):
        for b in range(ty):
            rows = []
            for c in range(3):
                row = c * tiles + a * ty + b
                rows.append(trade_p[row // per, row % per : row % per + 1, :])
            rows.append(jnp.full((1, beads), 1.0, jnp.float32))
            rows.append(jnp.zeros((4, beads), jnp.float32))
            pos = jnp.concatenate(rows, axis=0)
            pos2[a + 1, b + 1] = pos
            prepare(a + 1, b + 1, trade_h[a, b], pos)

    step(1, trade_h, rim2, pos2, noise2, finish_second, lambda g: None)
    for part in range(groups + 1):
        for k in range(1, reps):
            first_copy(part, k).wait_send()
            second_copy(part, k).wait_send()


def per_device(
    particle_descriptors,
    particle_locations_all,
    earlier_jitter,
    later_jitter,
    adjacent_tile_slots,
    thermal_levels,
    heat_slot_of_copy,
    partner_choice,
    normalizer_gain,
    query_lookup_matrix,
    message_output_matrix,
    lookup_charge_map,
    attention_head_falloff,
    attention_head_weight,
):
    _, tx, ty, beads, feats = particle_descriptors.shape
    reps, nx, ny = (lax.axis_size(axis) for axis in ("rep", "gx", "gy"))
    tiles, ext = tx * ty, (tx + 2) * (ty + 2)
    heads = attention_head_falloff.shape[0]
    slot_count = adjacent_tile_slots.shape[2]
    groups = 2
    piece = tiles * beads // groups // reps
    per = -(-3 * tiles // reps)
    vmem = pl.BlockSpec(memory_space=pltpu.VMEM)
    smem = pl.BlockSpec(memory_space=pltpu.SMEM)
    bf16, f32 = jnp.bfloat16, jnp.float32
    return pl.pallas_call(
        functools.partial(window_kernel, (reps, nx, ny)),
        out_shape=(
            jax.ShapeDtypeStruct(particle_descriptors.shape, bf16),
            jax.ShapeDtypeStruct(particle_locations_all.shape, f32),
            jax.ShapeDtypeStruct(particle_locations_all.shape, f32),
        ),
        in_specs=[vmem, vmem, vmem, vmem, smem, smem, smem, smem, vmem, vmem, vmem, vmem, smem, smem],
        out_specs=(vmem, vmem, vmem),
        scratch_shapes=[
            pltpu.VMEM((ext, beads, feats), bf16),
            pltpu.VMEM((ext, beads, 2 * feats), bf16),
            pltpu.VMEM((ext, 8, beads), f32),
            pltpu.VMEM((tiles, beads, feats), bf16),
            pltpu.VMEM((tiles, heads * beads, slot_count * beads), bf16),
            pltpu.VMEM((tx + 2, ty + 2, beads, feats), bf16),
            pltpu.VMEM((tx + 2, ty + 2, beads, feats), bf16),
            pltpu.VMEM((tx + 2, ty + 2, 8, beads), f32),
            pltpu.VMEM((tx + 2, ty + 2, 8, beads), f32),
            pltpu.VMEM((groups, reps, piece, feats), bf16),
            pltpu.VMEM((reps, per, beads), f32),
            pltpu.VMEM((reps, piece, feats), bf16),
            pltpu.VMEM((reps, piece, feats), bf16),
            pltpu.VMEM((reps, per, beads), f32),
            pltpu.VMEM((groups, reps, piece, feats), bf16),
            pltpu.VMEM((reps, per, beads), f32),
            pltpu.VMEM((tx, ty, beads, feats), bf16),
            pltpu.VMEM((reps, per, beads), f32),
            pltpu.SemaphoreType.DMA((2, len(DIRECTIONS), 2)),
            pltpu.SemaphoreType.DMA((2, len(DIRECTIONS), 2)),
            pltpu.SemaphoreType.DMA((2, groups + 1, reps)),
            pltpu.SemaphoreType.DMA((2, groups + 1, reps)),
        ],
        compiler_params=pltpu.CompilerParams(
            collective_id=0, has_side_effects=True, vmem_limit_bytes=48 * 2**20
        ),
    )(
        particle_descriptors,
        particle_locations_all,
        earlier_jitter,
        later_jitter,
        adjacent_tile_slots,
        thermal_levels,
        heat_slot_of_copy,
        partner_choice,
        normalizer_gain.reshape(1, feats),
        query_lookup_matrix,
        message_output_matrix,
        lookup_charge_map.reshape(1, feats),
        attention_head_falloff,
        attention_head_weight,
    )


def solution(mesh):
    in_specs = (
        P("rep", "gx", "gy", None, None),
        P("rep", None, "gx", "gy", None),
        P("rep", None, "gx", "gy", None),
        P("rep", None, "gx", "gy", None),
        P("gx", "gy", None),
        P(),
        P("rep"),
        P(),
        P(),
        P(),
        P(),
        P(),
        P(),
        P(),
    )
    out_specs = (
        P("rep", "gx", "gy", None, None),
        P("rep", None, "gx", "gy", None),
        P("rep", None, "gx", "gy", None),
    )
    return jax.shard_map(
        per_device, mesh=mesh, in_specs=in_specs, out_specs=out_specs, check_vma=False
    )
```

time: 119 us -> 48.6 us (0.41)
  starting transfers between devices: 59.3 us -> 0 us
  waiting for transfers between devices: 23.2 us -> 0 us
  Pallas kernels: 20.5 us -> 39.7 us
  local copies, waits for them, and re-layouts: 10.1 us -> 7.12 us
  other arithmetic: 2.67 us -> 0 us
    ppermute x16 -> x0, starting transfers between devices: 40.6 us -> none  [the longest x8 30.3 us: with_halo(): lax.ppermute(tail, axis, [(i, (i + 1) % count) for i in range(ends)])]
    pallas_call x2 -> x1, Pallas kernels: 20.5 us -> 39.7 us  [per_device(): pl.pallas_call(functools.partial(window_kernel, (reps, nx, ny)), out_shap...]
    all_to_all x4 -> x0, starting transfers between devices: 18.7 us -> none  [the longest x2 10.4 us: trade(): lax.all_to_all(values.reshape(flat), 'rep', split_axis=1, concat_axis=1,...]
    all_to_all x4 -> x0, waiting for transfers between devices: 16 us -> none  [the longest x2 8.6 us: trade(): lax.all_to_all(jnp.take(spread, partner_choice, axis=1), 'rep', split_axi...]
    ppermute x16 -> x0, waiting for transfers between devices: 7.21 us -> none  [the longest x8 4.57 us: with_halo(): lax.ppermute(head, axis, [((i + 1) % count, i) for i in range(ends)])]
    unnamed x38 -> x29, local copies, waits for them, and re-layouts: 5.15 us -> 7.12 us
    all_to_all x2 -> x0, other arithmetic: 1.34 us -> none  [the longest x1 0.67 us: trade(): lax.all_to_all(jnp.take(spread, partner_choice, axis=1), 'rep', split_axi...]
    gather x2 -> x0, local copies, waits for them, and re-layouts: 1.22 us -> none  [trade(): jnp.take(spread, partner_choice, axis=1)]
  transfers between devices with their start and end apart: 20 -> 0, of which waited for: 9 -> 0; matrix products, arithmetic and copies ran while one was open for 4% -> 0% of each run, Pallas kernels for 0% -> 0%
where the time goes in v2:
time: 48.6 us; the launch traced here: 48.3 us
  Pallas kernels  39.7 us (82%)
  local copies, waits for them, and re-layouts  7.12 us (15%)
  between operations  1.4 us (3%)
    pallas_call x1, Pallas kernels, per_device(): pl.pallas_call(functools.partial(window_kernel, (reps, nx, ny)), out_shap...  39.7 us
    unnamed x29, local copies, waits for them, and re-layouts  7.12 us

profile of v2, /device:TPU:0, one launch (start us, length us, event | category | flops | bytes accessed | tf_op | source)
XLA Modules:
  0.0 48.3 jit_solution(13786872225308911862)
XLA Ops:
  0.6 0.0 copy-start.10
  0.6 0.0 copy-start.11
  0.7 0.0 copy-start.12
  1.3 0.0 copy-start.6
  1.3 0.0 copy-start.7
  1.4 0.0 copy-start.8
  1.4 0.0 copy-start.9
  1.4 0.0 copy-done.10
  1.4 0.0 copy-done.11
  1.4 0.0 copy-done.12
  1.4 0.6 %copy-done.6 = s32[2,2,6]{2,1,0:T(2,128)S(1)} copy-done((s32[2,2,6]{2,1,0:T(2,128)S(1)}, s32[2,2,6]{2,1,0:T(2,128)}, u32[]{:S(2)}) %copy-start.6) | copy-done | bytes 120
  2.0 0.0 copy-done.7
  2.0 0.0 copy-done.8
  2.0 0.0 copy-done.9
  2.0 0.0 copy-start
  2.0 0.9 %copy-done = bf16[1,2,2,128,128]{4,3,2,1,0:T(8,128)(2,1)S(1)} copy-done((bf16[1,2,2,128,128]{4,3,2,1,0:T(8,128)(2,1)S(1)}, bf16[1,2,2,128,128]{4,3,2,1,0:T(8,128)(2,1)}, u32[]{:S(2)}) %copy-start) | copy-done | bytes 131096
  2.9 0.0 copy-start.1
  2.9 0.9 %copy-done.1 = bf16[128,384]{1,0:T(8,128)(2,1)S(1)} copy-done((bf16[128,384]{1,0:T(8,128)(2,1)S(1)}, bf16[128,384]{1,0:T(8,128)(2,1)}, u32[]{:S(2)}) %copy-start.1) | copy-done | bytes 98328
  3.8 0.0 copy-start.2
  3.8 0.8 %copy-done.2 = bf16[128,128]{1,0:T(8,128)(2,1)S(1)} copy-done((bf16[128,128]{1,0:T(8,128)(2,1)S(1)}, bf16[128,128]{1,0:T(8,128)(2,1)}, u32[]{:S(2)}) %copy-start.2) | copy-done | bytes 32792
  4.6 0.0 copy-start.3
  4.6 0.7 %copy-done.3 = f32[1,3,2,2,128]{4,3,2,1,0:T(2,128)S(1)} copy-done((f32[1,3,2,2,128]{4,3,2,1,0:T(2,128)S(1)}, f32[1,3,2,2,128]{4,3,2,1,0:T(2,128)}, u32[]{:S(2)}) %copy-start.3) | copy-done | bytes 6168
  5.3 0.0 copy-start.4
  5.3 0.7 %copy-done.4 = f32[1,3,2,2,128]{4,3,2,1,0:T(2,128)S(1)} copy-done((f32[1,3,2,2,128]{4,3,2,1,0:T(2,128)S(1)}, f32[1,3,2,2,128]{4,3,2,1,0:T(2,128)}, u32[]{:S(2)}) %copy-start.4) | copy-done | bytes 6168
  6.0 0.0 copy-start.5
  6.0 0.7 %copy-done.5 = f32[1,3,2,2,128]{4,3,2,1,0:T(2,128)S(1)} copy-done((f32[1,3,2,2,128]{4,3,2,1,0:T(2,128)S(1)}, f32[1,3,2,2,128]{4,3,2,1,0:T(2,128)}, u32[]{:S(2)}) %copy-start.5) | copy-done | bytes 6168
  6.7 39.7 %shard_map.157 = (bf16[1,2,2,128,128]{4,3,2,1,0:T(8,128)(2,1)S(1)}, f32[1,3,2,2,128]{4,3,2,1,0:T(2,128)S(1)}, f32[1,3,2,2,128]{4,3,2,1,0:T(2,128)S(1)}) custom-call(bf16[1,2,2,128,128]{4,3,2,1,0:T(8,128)(2,1)S(1)} %copy-done, f32[1,3,2,2,128]{4,3,2,1,0:T(2,128)S(1)} %copy-done.3, f32[1,3,2,2,128]{4,3,2,1,0:T(2,128)S(1)} %copy-done.4, ...), custom_call_target="tpu_custom_call" | custom-call | tf_op jit(solution)/shard_map/pallas_call | solution.py:393
  46.4 0.7 %copy.21 = bf16[1,2,2,128,128]{4,3,2,1,0:T(8,128)(2,1)} copy(bf16[1,2,2,128,128]{4,3,2,1,0:T(8,128)(2,1)S(1)} %get-tuple-element.6) | data formatting | bytes 262144
  47.1 0.6 %copy.22 = f32[1,3,2,2,128]{4,3,2,1,0:T(2,128)} copy(f32[1,3,2,2,128]{4,3,2,1,0:T(2,128)S(1)} %get-tuple-element.7) | data formatting | bytes 12288
  47.7 0.6 %copy.23 = f32[1,3,2,2,128]{4,3,2,1,0:T(2,128)} copy(f32[1,3,2,2,128]{4,3,2,1,0:T(2,128)S(1)} %get-tuple-element.8) | data formatting | bytes 12288
Async XLA Ops:
  0.6 0.7 %copy-start.10 = (bf16[128]{0:T(256)(128)(2,1)S(1)}, bf16[128]{0:T(256)(128)(2,1)}, u32[]{:S(2)}) copy-start(bf16[128]{0:T(256)(128)(2,1)} %param.25) | copy-start | bytes 772
  0.6 0.7 %copy-start.11 = (f32[8]{0:T(128)S(1)}, f32[8]{0:T(128)}, u32[]{:S(2)}) copy-start(f32[8]{0:T(128)} %falloff.1) | copy-start | bytes 100
  0.7 0.7 %copy-start.12 = (f32[8]{0:T(128)S(1)}, f32[8]{0:T(128)}, u32[]{:S(2)}) copy-start(f32[8]{0:T(128)} %mixing.1) | copy-start | bytes 100
  1.3 0.7 %copy-start.6 = (s32[2,2,6]{2,1,0:T(2,128)S(1)}, s32[2,2,6]{2,1,0:T(2,128)}, u32[]{:S(2)}) copy-start(s32[2,2,6]{2,1,0:T(2,128)} %slots.1) | copy-start | bytes 292
  1.3 0.7 %copy-start.7 = (f32[8]{0:T(128)S(1)}, f32[8]{0:T(128)}, u32[]{:S(2)}) copy-start(f32[8]{0:T(128)} %levels.1) | copy-start | bytes 100
  1.4 0.7 %copy-start.8 = (s32[8]{0:T(128)S(1)}, s32[8]{0:T(128)}, u32[]{:S(2)}) copy-start(s32[8]{0:T(128)} %partner.1) | copy-start | bytes 100
  1.4 0.7 %copy-start.9 = (f32[128]{0:T(128)S(1)}, f32[128]{0:T(128)}, u32[]{:S(2)}) copy-start(f32[128]{0:T(128)} %param.22) | copy-start | bytes 1540
  2.0 0.9 %copy-start = (bf16[1,2,2,128,128]{4,3,2,1,0:T(8,128)(2,1)S(1)}, bf16[1,2,2,128,128]{4,3,2,1,0:T(8,128)(2,1)}, u32[]{:S(2)}) copy-start(bf16[1,2,2,128,128]{4,3,2,1,0:T(8,128)(2,1)} %h_in.1) | copy-start | bytes 393220
  2.9 0.9 %copy-start.1 = (bf16[128,384]{1,0:T(8,128)(2,1)S(1)}, bf16[128,384]{1,0:T(8,128)(2,1)}, u32[]{:S(2)}) copy-start(bf16[128,384]{1,0:T(8,128)(2,1)} %weight.1) | copy-start | bytes 294916
  3.8 0.8 %copy-start.2 = (bf16[128,128]{1,0:T(8,128)(2,1)S(1)}, bf16[128,128]{1,0:T(8,128)(2,1)}, u32[]{:S(2)}) copy-start(bf16[128,128]{1,0:T(8,128)(2,1)} %out_weight.1) | copy-start | bytes 98308
  4.6 0.7 %copy-start.3 = (f32[1,3,2,2,128]{4,3,2,1,0:T(2,128)S(1)}, f32[1,3,2,2,128]{4,3,2,1,0:T(2,128)}, u32[]{:S(2)}) copy-start(f32[1,3,2,2,128]{4,3,2,1,0:T(2,128)} %p_in.1) | copy-start | bytes 18436
  5.3 0.7 %copy-start.4 = (f32[1,3,2,2,128]{4,3,2,1,0:T(2,128)S(1)}, f32[1,3,2,2,128]{4,3,2,1,0:T(2,128)}, u32[]{:S(2)}) copy-start(f32[1,3,2,2,128]{4,3,2,1,0:T(2,128)} %noise1.1) | copy-start | bytes 18436
  6.0 0.7 %copy-start.5 = (f32[1,3,2,2,128]{4,3,2,1,0:T(2,128)S(1)}, f32[1,3,2,2,128]{4,3,2,1,0:T(2,128)}, u32[]{:S(2)}) copy-start(f32[1,3,2,2,128]{4,3,2,1,0:T(2,128)} %noise2.1) | copy-start | bytes 18436

commit v3 on v2

--- a/solution.py
+++ b/solution.py
@@ -25,6 +25,7 @@
 
 
 WINDOW = window_coefficients(4)
+CHUNK = 32
 
 
 def project(h, gain_row, weight):
@@ -41,21 +42,24 @@
     return jnp.concatenate([block, jnp.zeros((lanes - rows, lanes), block.dtype)], axis=0)
 
 
-def prepare_tile(t, h, pos, gain_row, weight, charge, k_ref, rhs_ref, near_ref):
+def prepare_features(t, h, gain_row, weight, k_ref, rhs_ref):
     feats = h.shape[1]
     proj = project(h, gain_row, weight)
-    keys = proj[:, feats : 2 * feats]
+    k_ref[t] = proj[:, feats : 2 * feats]
+    rhs_ref[t, :, :feats] = proj[:, 2 * feats :]
+    return proj[:, :feats]
+
+
+def prepare_force(t, pos, charge, k_ref, rhs_ref, near_ref):
+    feats = charge.shape[1]
     near_ref[t] = pos
-    k_ref[t] = keys
-    rhs_ref[t, :, :feats] = proj[:, 2 * feats :]
     probe = lax.dot_general(
-        charge, keys, (((1,), (1,)), ((), ())), preferred_element_type=jnp.float32
+        charge, k_ref[t], (((1,), (1,)), ((), ())), preferred_element_type=jnp.float32
     )
     rows = probe * pos
     high = rows.astype(jnp.bfloat16).astype(jnp.float32)
     columns = tall(jnp.concatenate([high, rows - high], axis=0)).T
     rhs_ref[t, :, feats:] = columns.astype(jnp.bfloat16)
-    return proj[:, :feats]
 
 
 def score_slots(i, group, own, q, pos, slot_of, work, s_ref, falloff):
@@ -64,50 +68,60 @@
     heads = falloff.shape[0]
     lane = lax.broadcasted_iota(jnp.int32, (beads, feats), 1) // (feats // heads)
     zero = jnp.zeros_like(q)
-    stacked = jnp.concatenate([jnp.where(lane == e, q, zero) for e in range(heads)], axis=0)
+    masked = [jnp.where(lane == e, q, zero) for e in range(heads)]
+    chunks = range(0, beads, CHUNK)
+    stacked = jnp.concatenate([m[r : r + CHUNK] for r in chunks for m in masked], axis=0)
     columns = tall(pos).T
+    rates = [falloff[e] * -LOG2E for e in range(heads)]
     for part in group:
         where = [jnp.where(slot_of(n) >= 0, slot_of(n), own) for n in part]
         present = [(slot_of(n) >= 0).astype(jnp.float32) for n in part]
         keys = join([k_ref[w] for w in where], 0)
         logits = lax.dot_general(
             stacked, keys, (((1,), (1,)), ((), ())), preferred_element_type=jnp.float32
-        )
+        ).astype(jnp.bfloat16)
         near = join([near_ref[w] for w in where], 1)
         occupied = join([jnp.full((1, beads), v, jnp.float32) for v in present], 1)
-        squared = None
-        for c in range(3):
-            offset = columns[:, c : c + 1] - near[c : c + 1, :]
-            squared = offset * offset if squared is None else squared + offset * offset
-        squared = jnp.minimum(squared, 1.0)
-        window = jnp.full_like(squared, WINDOW[0])
-        for coefficient in WINDOW[1:]:
-            window = window * squared + coefficient
-        window = window * (1.0 - squared)
-        window = window * window * occupied
-        for e in range(heads):
-            half = logits[e * beads : (e + 1) * beads]
-            act = half + half * jnp.tanh(half)
-            score = act * (window * jnp.exp2(squared * (falloff[e] * -LOG2E)))
-            s_ref[i, e * beads : (e + 1) * beads, part[0] * beads : (part[-1] + 1) * beads] = (
-                score.astype(jnp.bfloat16)
-            )
+        for r in chunks:
+            squared = None
+            for c in range(3):
+                offset = columns[r : r + CHUNK, c : c + 1] - near[c : c + 1, :]
+                squared = offset * offset if squared is None else squared + offset * offset
+            squared = jnp.minimum(squared, 1.0)
+            window = jnp.full_like(squared, WINDOW[0])
+            for coefficient in WINDOW[1:]:
+                window = window * squared + coefficient
+            window = window * (1.0 - squared)
+            window = (window * window * occupied).astype(jnp.bfloat16)
+            for e in range(heads):
+                start = r * heads + e * CHUNK
+                half = logits[start : start + CHUNK]
+                act = half + half * jnp.tanh(half)
+                decay = jnp.exp2((squared * rates[e]).astype(jnp.bfloat16))
+                s_ref[i, start : start + CHUNK, part[0] * beads : (part[-1] + 1) * beads] = act * (
+                    window * decay
+                )
 
 
 def finish_tile(i, own, h, pos, noise, scale, slot_of, slot_count, work, s_ref, mixing, out_weight):
     beads, feats = h.shape
     heads = mixing.shape[0]
-    lane = lax.broadcasted_iota(jnp.int32, (beads, feats), 1) // (feats // heads)
+    lane = lax.broadcasted_iota(jnp.int32, (CHUNK, feats), 1) // (feats // heads)
     where = [jnp.where(slot_of(n) >= 0, slot_of(n), own) for n in range(slot_count)]
     rhs = jnp.concatenate([work.rhs[w] for w in where], axis=0)
     sums = jnp.dot(s_ref[i], rhs, preferred_element_type=jnp.float32)
-    message = jnp.zeros((beads, feats), jnp.float32)
-    pulls = jnp.zeros((beads, feats), jnp.float32)
-    for e in range(heads):
-        part = sums[e * beads : (e + 1) * beads]
-        message = jnp.where(lane == e, part[:, :feats], message)
-        pulls = pulls + mixing[e] * part[:, feats:]
-    message = (message * MESSAGE_SCALE).astype(jnp.bfloat16)
+    messages, pulls = [], []
+    for r in range(0, beads, CHUNK):
+        message = jnp.zeros((CHUNK, feats), jnp.float32)
+        pull = jnp.zeros((CHUNK, feats), jnp.float32)
+        for e in range(heads):
+            part = sums[r * heads + e * CHUNK : r * heads + (e + 1) * CHUNK]
+            message = jnp.where(lane == e, part[:, :feats], message)
+            pull = pull + mixing[e] * part[:, feats:]
+        messages.append(message)
+        pulls.append(pull)
+    message = (jnp.concatenate(messages, axis=0) * MESSAGE_SCALE).astype(jnp.bfloat16)
+    pulls = jnp.concatenate(pulls, axis=0)
     mixed = jnp.dot(message, out_weight, preferred_element_type=jnp.float32)
     updated = (h.astype(jnp.float32) + mixed).astype(jnp.bfloat16)
     turned = pulls.T
@@ -129,6 +143,9 @@
     return jnp.concatenate(rows, axis=0)
 
 
+OPERANDS = 14
+
+
 class Work:
     def __init__(self, k, rhs, near, q):
         self.k, self.rhs, self.near, self.q = k, rhs, near, q
@@ -143,8 +160,21 @@
     return (size - 1, 1, 0) if step > 0 else (0, 1, size + 1)
 
 
-def window_kernel(sizes, h_in, p_in, noise1, noise2, slots, levels, heat_slot, partner, gain, weight,
-                  out_weight, charge_ref, falloff, mixing, h_out, moved_out, force_out, k_ref,
+def window_kernel(sizes, *refs):
+    operands, refs = refs[:OPERANDS], refs[OPERANDS:]
+    outs, held, refs = refs[:3], refs[3 : 3 + OPERANDS], refs[3 + OPERANDS :]
+    load_sem, refs = refs[0], refs[1:]
+    loads = [
+        pltpu.make_async_copy(src, dst, load_sem.at[n])
+        for n, (src, dst) in enumerate(zip(operands, held))
+    ]
+    for load in loads:
+        load.start()
+    window_body(sizes, loads, *held, *outs, *refs)
+
+
+def window_body(sizes, loads, h_in, p_in, noise1, noise2, slots, levels, heat_slot, partner, gain,
+                  weight, out_weight, charge_ref, falloff, mixing, h_out, moved_out, force_out, k_ref,
                   rhs_ref, near_ref, q_ref, s_ref, rim1, rim2, pos1, pos2, mine_h, mine_p, spread_a,
                   spread_b, spread_p, route_h, route_p, trade_h, trade_p, halo_send, halo_recv,
                   swap_send, swap_recv):
@@ -155,7 +185,6 @@
     slot_count = slots.shape[2]
     me, gx, gy = lax.axis_index("rep"), lax.axis_index("gx"), lax.axis_index("gy")
     work = Work(k_ref, rhs_ref, near_ref, q_ref)
-    scale = jnp.sqrt(jnp.full((1, beads), levels[heat_slot[0]], jnp.float32))
     spread_h = (spread_a, spread_b)
     groups = len(spread_h)
     piece = tiles * beads // groups // reps
@@ -181,28 +210,34 @@
             pl.semaphore_signal(barrier, inc=1, device_id=(me, gx + dx, gy + dy),
                                 device_id_type=pl.DeviceIdType.MESH)
 
+    for load in loads:
+        load.wait()
+    scale = jnp.sqrt(jnp.full((1, beads), levels[heat_slot[0]], jnp.float32))
     gain_row, weights, out_w = gain[...], weight[...], out_weight[...]
     charge = jnp.broadcast_to(charge_ref[...].astype(jnp.float32), (8, feats)).astype(jnp.bfloat16)
 
-    def prepare(row, col, h, pos):
-        q = prepare_tile(row * ey + col, h, pos, gain_row, weights, charge, k_ref, rhs_ref, near_ref)
+    def prepare_pos(row, col, pos):
+        prepare_force(row * ey + col, pos, charge, k_ref, rhs_ref, near_ref)
+
+    def prepare(row, col, h):
+        q = prepare_features(row * ey + col, h, gain_row, weights, k_ref, rhs_ref)
         if 1 <= row <= tx and 1 <= col <= ty:
             q_ref[(row - 1) * ty + col - 1] = q * jnp.bfloat16(0.125)
 
-    def halo_copies(step, d, h_src, rim, pos):
+    def halo_copy(step, d, kind, h_src, rim, pos):
         dx, dy = DIRECTIONS[d]
         (r0, nr, r1), (c0, nc, c1) = side(dx, tx), side(dy, ty)
         target = (me, gx + dx, gy + dy)
-        return [
-            pltpu.make_async_remote_copy(
-                src_ref=src, dst_ref=dst, send_sem=halo_send.at[step, d, kind],
-                recv_sem=halo_recv.at[step, d, kind], device_id=target,
-                device_id_type=pl.DeviceIdType.MESH)
-            for kind, (src, dst) in enumerate((
-                (h_src.at[pl.ds(r0, nr), pl.ds(c0, nc)], rim.at[pl.ds(r1, nr), pl.ds(c1, nc)]),
-                (pos.at[pl.ds(r0 + 1, nr), pl.ds(c0 + 1, nc)], pos.at[pl.ds(r1, nr), pl.ds(c1, nc)]),
-            ))
-        ]
+        if kind == 0:
+            src = h_src.at[pl.ds(r0, nr), pl.ds(c0, nc)]
+            dst = rim.at[pl.ds(r1, nr), pl.ds(c1, nc)]
+        else:
+            src = pos.at[pl.ds(r0 + 1, nr), pl.ds(c0 + 1, nc)]
+            dst = pos.at[pl.ds(r1, nr), pl.ds(c1, nc)]
+        return pltpu.make_async_remote_copy(
+            src_ref=src, dst_ref=dst, send_sem=halo_send.at[step, d, kind],
+            recv_sem=halo_recv.at[step, d, kind], device_id=target,
+            device_id_type=pl.DeviceIdType.MESH)
 
     def slot_reader(i):
         return lambda n: slots[i // ty, lax.rem(i, ty), n]
@@ -210,13 +245,13 @@
     def own_of(i):
         return (i // ty + 1) * ey + lax.rem(i, ty) + 1
 
-    def step(number, h_src, rim, pos, noise, finish, after_group):
+    def start_halo(number, kind, h_src, rim, pos):
         for d, (dx, dy) in enumerate(DIRECTIONS):
             @pl.when(has(dx, dy))
             def _(d=d):
-                for copy in halo_copies(number, d, h_src, rim, pos):
-                    copy.start()
-
+                halo_copy(number, d, kind, h_src, rim, pos).start()
+
+    def step(number, h_src, rim, pos, noise, finish, cuts, after_cut):
         def self_body(i, carry):
             score_slots(i, ((0,),), own_of(i), q_ref[i], near_ref[own_of(i)], slot_reader(i), work,
                         s_ref, falloff)
@@ -226,12 +261,13 @@
         for d, (dx, dy) in enumerate(DIRECTIONS):
             @pl.when(has(-dx, -dy))
             def _(d=d, dx=dx, dy=dy):
-                for copy in halo_copies(number, d, h_src, rim, pos):
-                    copy.wait_recv()
+                for kind in range(2):
+                    halo_copy(number, d, kind, h_src, rim, pos).wait_recv()
                 (_, nr, r1), (_, nc, c1) = side(dx, tx), side(dy, ty)
                 for row in range(r1, r1 + nr):
                     for col in range(c1, c1 + nc):
-                        prepare(row, col, rim[row, col], pos[row, col])
+                        prepare(row, col, rim[row, col])
+                        prepare_pos(row, col, pos[row, col])
 
         rest = [(n, n + 1) if n + 1 < slot_count else (n,) for n in range(1, slot_count, 2)]
 
@@ -244,14 +280,14 @@
                 slot_count, work, s_ref, mixing, out_w))
             return carry
 
-        for g in range(groups):
-            lax.fori_loop(g * tiles // groups, (g + 1) * tiles // groups, body, 0)
-            after_group(g)
+        for first, last in zip(cuts[:-1], cuts[1:]):
+            lax.fori_loop(first, last, body, 0)
+            after_cut(last)
         for d, (dx, dy) in enumerate(DIRECTIONS):
             @pl.when(has(dx, dy))
             def _(d=d):
-                for copy in halo_copies(number, d, h_src, rim, pos):
-                    copy.wait_send()
+                for kind in range(2):
+                    halo_copy(number, d, kind, h_src, rim, pos).wait_send()
 
     def swap_copy(phase, part, k, src, dst):
         return pltpu.make_async_remote_copy(
@@ -314,13 +350,16 @@
             row = c * tiles + i
             mine_p[row // per, pl.ds(lax.rem(row, per), 1), :] = moved[c : c + 1]
 
-    def after_first(g):
-        send_first(g)
-        if g:
+    def after_first(done):
+        if done == tiles // groups:
+            send_first(0)
+        elif done < tiles:
+            send_second(0)
+        else:
             send_first(groups)
-        if g:
-            for part in range(groups + 1):
-                send_second(part)
+            send_first(1)
+            send_second(groups)
+            send_second(1)
 
     def finish_second(i, a, b, updated, moved, force):
         h_out[0, a, b] = updated
@@ -328,35 +367,51 @@
             moved_out[0, c, a, pl.ds(b, 1), :] = moved[c : c + 1]
             force_out[0, c, a, pl.ds(b, 1), :] = force[c : c + 1]
 
-    for a in range(tx):
-        for b in range(ty):
-            pos = rows_of(p_in, a, b, 1.0)
-            pos1[a + 1, b + 1] = pos
-            prepare(a + 1, b + 1, h_in[0, a, b], pos)
+    grid = [(a, b) for a in range(tx) for b in range(ty)]
+    half_tiles = tiles // groups
+    for a, b in grid:
+        pos1[a + 1, b + 1] = rows_of(p_in, a, b, 1.0)
+    for a, b in grid[:half_tiles]:
+        prepare(a + 1, b + 1, h_in[0, a, b])
     mine_p[...] = jnp.zeros_like(mine_p)
 
     columns = 1 + jnp.minimum(gx, 1) + jnp.minimum(nx - 1 - gx, 1)
     lines = 1 + jnp.minimum(gy, 1) + jnp.minimum(ny - 1 - gy, 1)
     pl.semaphore_wait(barrier, reps - 2 + columns * lines)
 
-    step(0, h_in.at[0], rim1, pos1, noise1, finish_first, after_first)
-
-    for part in range(groups + 1):
+    for kind in range(2):
+        start_halo(0, kind, h_in.at[0], rim1, pos1)
+    for a, b in grid[half_tiles:]:
+        prepare(a + 1, b + 1, h_in[0, a, b])
+    for a, b in grid:
+        prepare_pos(a + 1, b + 1, rows_of(p_in, a, b, 1.0))
+    cuts = (0, half_tiles, tiles - 1, tiles)
+    step(0, h_in.at[0], rim1, pos1, noise1, finish_first, cuts, after_first)
+
+    def arrive(part):
         for k in range(1, reps):
             second_copy(part, k).wait_recv()
-    for a in range(tx):
-        for b in range(ty):
-            rows = []
-            for c in range(3):
-                row = c * tiles + a * ty + b
-                rows.append(trade_p[row // per, row % per : row % per + 1, :])
-            rows.append(jnp.full((1, beads), 1.0, jnp.float32))
-            rows.append(jnp.zeros((4, beads), jnp.float32))
-            pos = jnp.concatenate(rows, axis=0)
-            pos2[a + 1, b + 1] = pos
-            prepare(a + 1, b + 1, trade_h[a, b], pos)
-
-    step(1, trade_h, rim2, pos2, noise2, finish_second, lambda g: None)
+
+    arrive(0)
+    for a, b in grid[:half_tiles]:
+        prepare(a + 1, b + 1, trade_h[a, b])
+    arrive(groups)
+    for a, b in grid:
+        rows = []
+        for c in range(3):
+            row = c * tiles + a * ty + b
+            rows.append(trade_p[row // per, row % per : row % per + 1, :])
+        rows.append(jnp.full((1, beads), 1.0, jnp.float32))
+        rows.append(jnp.zeros((4, beads), jnp.float32))
+        pos2[a + 1, b + 1] = jnp.concatenate(rows, axis=0)
+    start_halo(1, 1, trade_h, rim2, pos2)
+    arrive(1)
+    start_halo(1, 0, trade_h, rim2, pos2)
+    for a, b in grid[half_tiles:]:
+        prepare(a + 1, b + 1, trade_h[a, b])
+    for a, b in grid:
+        prepare_pos(a + 1, b + 1, pos2[a + 1, b + 1])
+    step(1, trade_h, rim2, pos2, noise2, finish_second, (0, tiles), lambda done: None)
     for part in range(groups + 1):
         for k in range(1, reps):
             first_copy(part, k).wait_send()
@@ -388,8 +443,23 @@
     piece = tiles * beads // groups // reps
     per = -(-3 * tiles // reps)
     vmem = pl.BlockSpec(memory_space=pltpu.VMEM)
-    smem = pl.BlockSpec(memory_space=pltpu.SMEM)
     bf16, f32 = jnp.bfloat16, jnp.float32
+    operands = (
+        particle_descriptors,
+        particle_locations_all,
+        earlier_jitter,
+        later_jitter,
+        adjacent_tile_slots,
+        thermal_levels,
+        heat_slot_of_copy,
+        partner_choice,
+        normalizer_gain.reshape(1, feats),
+        query_lookup_matrix,
+        message_output_matrix,
+        lookup_charge_map.reshape(1, feats),
+        attention_head_falloff,
+        attention_head_weight,
+    )
     return pl.pallas_call(
         functools.partial(window_kernel, (reps, nx, ny)),
         out_shape=(
@@ -397,9 +467,14 @@
             jax.ShapeDtypeStruct(particle_locations_all.shape, f32),
             jax.ShapeDtypeStruct(particle_locations_all.shape, f32),
         ),
-        in_specs=[vmem, vmem, vmem, vmem, smem, smem, smem, smem, vmem, vmem, vmem, vmem, smem, smem],
+        in_specs=[pl.BlockSpec(memory_space=pltpu.HBM)] * OPERANDS,
         out_specs=(vmem, vmem, vmem),
         scratch_shapes=[
+            (pltpu.SMEM if n in (4, 5, 6, 7, 12, 13) else pltpu.VMEM)(x.shape, x.dtype)
+            for n, x in enumerate(operands)
+        ]
+        + [
+            pltpu.SemaphoreType.DMA((OPERANDS,)),
             pltpu.VMEM((ext, beads, feats), bf16),
             pltpu.VMEM((ext, beads, 2 * feats), bf16),
             pltpu.VMEM((ext, 8, beads), f32),
@@ -424,24 +499,9 @@
             pltpu.SemaphoreType.DMA((2, groups + 1, reps)),
         ],
         compiler_params=pltpu.CompilerParams(
-            collective_id=0, has_side_effects=True, vmem_limit_bytes=48 * 2**20
+            collective_id=0, has_side_effects=True, vmem_limit_bytes=60 * 2**20
         ),
-    )(
-        particle_descriptors,
-        particle_locations_all,
-        earlier_jitter,
-        later_jitter,
-        adjacent_tile_slots,
-        thermal_levels,
-        heat_slot_of_copy,
-        partner_choice,
-        normalizer_gain.reshape(1, feats),
-        query_lookup_matrix,
-        message_output_matrix,
-        lookup_charge_map.reshape(1, feats),
-        attention_head_falloff,
-        attention_head_weight,
-    )
+    )(*operands)
 
 
 def solution(mesh):

time: 48.6 us -> 44.9 us (0.924)
  local copies, waits for them, and re-layouts: 7.12 us -> 2.87 us
  Pallas kernels: 39.7 us -> 40.5 us
    unnamed x29 -> x7, local copies, waits for them, and re-layouts: 7.12 us -> 2.87 us
    pallas_call x1, Pallas kernels: 39.7 us -> 40.5 us  [per_device(): pl.pallas_call(functools.partial(window_kernel, (reps, nx, ny)), out_shap...]
where the time goes in v3:
time: 44.9 us; the launch traced here: 44.7 us
  Pallas kernels  40.5 us (90%)
  local copies, waits for them, and re-layouts  2.87 us (6%)
  between operations  1.3 us (3%)
    pallas_call x1, Pallas kernels, per_device(): pl.pallas_call(functools.partial(window_kernel, (reps, nx, ny)), out_shap...  40.5 us
    unnamed x7, local copies, waits for them, and re-layouts  2.87 us

profile of v3, /device:TPU:0, one launch (start us, length us, event | category | flops | bytes accessed | tf_op | source)
XLA Modules:
  0.0 44.7 jit_solution(16171746797985489780)
XLA Ops:
  1.3 40.5 %shard_map.157 = (bf16[1,2,2,128,128]{4,3,2,1,0:T(8,128)(2,1)}, f32[1,3,2,2,128]{4,3,2,1,0:T(2,128)}, f32[1,3,2,2,128]{4,3,2,1,0:T(2,128)}) custom-call(bf16[1,2,2,128,128]{4,3,2,1,0:T(8,128)(2,1)} %refs_0_.1, f32[1,3,2,2,128]{4,3,2,1,0:T(2,128)} %refs_1_.1, f32[1,3,2,2,128]{4,3,2,1,0:T(2,128)} %refs_2_.1, f32[1,3,2,2,128]{4,3,2,1,0:T(2,128)} %refs_3_.1, ...), custom_call_target="tpu_custom_call" | custom-call | tf_op jit(solution)/shard_map/pallas_call | solution.py:463
  41.8 0.0 copy-start.1
  41.8 1.6 %copy.21 = bf16[1,2,2,128,128]{4,3,2,1,0:T(8,128)(2,1)} copy(bf16[1,2,2,128,128]{4,3,2,1,0:T(8,128)(2,1)} %get-tuple-element.6) | data formatting | bytes 262144
  43.4 0.0 copy-done.1
  43.4 0.0 copy-start
  43.4 0.6 %copy.22 = f32[1,3,2,2,128]{4,3,2,1,0:T(2,128)} copy(f32[1,3,2,2,128]{4,3,2,1,0:T(2,128)S(1)} %copy-done.1) | data formatting | bytes 12288
  44.0 0.1 copy-done
  44.1 0.6 %copy.23 = f32[1,3,2,2,128]{4,3,2,1,0:T(2,128)} copy(f32[1,3,2,2,128]{4,3,2,1,0:T(2,128)S(1)} %copy-done) | data formatting | bytes 12288
Async XLA Ops:
  41.8 1.6 %copy-start.1 = (f32[1,3,2,2,128]{4,3,2,1,0:T(2,128)S(1)}, f32[1,3,2,2,128]{4,3,2,1,0:T(2,128)}, u32[]{:S(2)}) copy-start(f32[1,3,2,2,128]{4,3,2,1,0:T(2,128)} %get-tuple-element.7) | copy-start | bytes 18436
  43.4 0.7 %copy-start = (f32[1,3,2,2,128]{4,3,2,1,0:T(2,128)S(1)}, f32[1,3,2,2,128]{4,3,2,1,0:T(2,128)}, u32[]{:S(2)}) copy-start(f32[1,3,2,2,128]{4,3,2,1,0:T(2,128)} %get-tuple-element.8) | copy-start | bytes 18436

commit v4 on v3

--- a/solution.py
+++ b/solution.py
@@ -92,14 +92,14 @@
             for coefficient in WINDOW[1:]:
                 window = window * squared + coefficient
             window = window * (1.0 - squared)
-            window = (window * window * occupied).astype(jnp.bfloat16)
+            window = window * window * occupied
             for e in range(heads):
                 start = r * heads + e * CHUNK
                 half = logits[start : start + CHUNK]
                 act = half + half * jnp.tanh(half)
-                decay = jnp.exp2((squared * rates[e]).astype(jnp.bfloat16))
-                s_ref[i, start : start + CHUNK, part[0] * beads : (part[-1] + 1) * beads] = act * (
-                    window * decay
+                decay = window * jnp.exp2(squared * rates[e])
+                s_ref[i, start : start + CHUNK, part[0] * beads : (part[-1] + 1) * beads] = (
+                    act * decay.astype(jnp.bfloat16)
                 )
 
 
@@ -136,7 +136,7 @@
 
 
 def rows_of(ref, a, b, fill):
-    rows = [ref[0, c, a, pl.ds(b, 1), :] for c in range(3)]
+    rows = [ref[c, a, pl.ds(b, 1), :] for c in range(3)]
     beads = rows[0].shape[1]
     rows.append(jnp.full((1, beads), fill, jnp.float32))
     rows.append(jnp.zeros((4, beads), jnp.float32))
@@ -162,24 +162,27 @@
 
 def window_kernel(sizes, *refs):
     operands, refs = refs[:OPERANDS], refs[OPERANDS:]
-    outs, held, refs = refs[:3], refs[3 : 3 + OPERANDS], refs[3 + OPERANDS :]
+    outs, held, refs = refs[:3], refs[3 : OPERANDS + 2], refs[OPERANDS + 2 :]
     load_sem, refs = refs[0], refs[1:]
+    feats_of, noise = held[0], held[2]
+    places = [feats_of.at[pl.ds(0, 1)], held[1], noise.at[pl.ds(0, 1)], noise.at[pl.ds(1, 1)]]
     loads = [
         pltpu.make_async_copy(src, dst, load_sem.at[n])
-        for n, (src, dst) in enumerate(zip(operands, held))
+        for n, (src, dst) in enumerate(zip(operands, places + list(held[3:])))
     ]
     for load in loads:
         load.start()
     window_body(sizes, loads, *held, *outs, *refs)
 
 
-def window_body(sizes, loads, h_in, p_in, noise1, noise2, slots, levels, heat_slot, partner, gain,
+def window_body(sizes, loads, h_both, p_in, noise_both, slots, levels, heat_slot, partner, gain,
                   weight, out_weight, charge_ref, falloff, mixing, h_out, moved_out, force_out, k_ref,
-                  rhs_ref, near_ref, q_ref, s_ref, rim1, rim2, pos1, pos2, mine_h, mine_p, spread_a,
-                  spread_b, spread_p, route_h, route_p, trade_h, trade_p, halo_send, halo_recv,
+                  rhs_ref, near_ref, q_ref, s_ref, rim_both, pos_both, mine_h, mine_p, spread_a,
+                  spread_b, spread_p, route_h, route_p, trade_p, halo_send, halo_recv,
                   swap_send, swap_recv):
     reps, nx, ny = sizes
-    _, tx, ty, beads, feats = h_in.shape
+    _, tx, ty, beads, feats = h_both.shape
+    trade_h = h_both.at[1]
     tiles = tx * ty
     ex, ey = tx + 2, ty + 2
     slot_count = slots.shape[2]
@@ -216,18 +219,18 @@
     gain_row, weights, out_w = gain[...], weight[...], out_weight[...]
     charge = jnp.broadcast_to(charge_ref[...].astype(jnp.float32), (8, feats)).astype(jnp.bfloat16)
 
-    def prepare_pos(row, col, pos):
-        prepare_force(row * ey + col, pos, charge, k_ref, rhs_ref, near_ref)
-
-    def prepare(row, col, h):
-        q = prepare_features(row * ey + col, h, gain_row, weights, k_ref, rhs_ref)
-        if 1 <= row <= tx and 1 <= col <= ty:
+    def prepare(row, col, h, pos, inner):
+        t = row * ey + col
+        q = prepare_features(t, h, gain_row, weights, k_ref, rhs_ref)
+        if inner:
             q_ref[(row - 1) * ty + col - 1] = q * jnp.bfloat16(0.125)
-
-    def halo_copy(step, d, kind, h_src, rim, pos):
+        prepare_force(t, pos, charge, k_ref, rhs_ref, near_ref)
+
+    def halo_copy(step, d, kind):
         dx, dy = DIRECTIONS[d]
         (r0, nr, r1), (c0, nc, c1) = side(dx, tx), side(dy, ty)
         target = (me, gx + dx, gy + dy)
+        h_src, rim, pos = h_both.at[step], rim_both.at[step], pos_both.at[step]
         if kind == 0:
             src = h_src.at[pl.ds(r0, nr), pl.ds(c0, nc)]
             dst = rim.at[pl.ds(r1, nr), pl.ds(c1, nc)]
@@ -245,49 +248,77 @@
     def own_of(i):
         return (i // ty + 1) * ey + lax.rem(i, ty) + 1
 
-    def start_halo(number, kind, h_src, rim, pos):
+    def each_direction(act, sign):
         for d, (dx, dy) in enumerate(DIRECTIONS):
-            @pl.when(has(dx, dy))
+            @pl.when(has(sign * dx, sign * dy))
             def _(d=d):
-                halo_copy(number, d, kind, h_src, rim, pos).start()
-
-    def step(number, h_src, rim, pos, noise, finish, cuts, after_cut):
+                for kind in range(2):
+                    act(d, kind)
+
+    def step(number):
+        each_direction(lambda d, kind: halo_copy(number, d, kind).start(), 1)
+
+        def inner_body(a, carry):
+            for b in range(ty):
+                prepare(a + 1, b + 1, h_both[number, a, b], pos_both[number, a + 1, b + 1], True)
+            return carry
+
+        lax.fori_loop(0, tx, inner_body, 0)
+
         def self_body(i, carry):
             score_slots(i, ((0,),), own_of(i), q_ref[i], near_ref[own_of(i)], slot_reader(i), work,
                         s_ref, falloff)
             return carry
 
         lax.fori_loop(0, tiles, self_body, 0)
-        for d, (dx, dy) in enumerate(DIRECTIONS):
-            @pl.when(has(-dx, -dy))
-            def _(d=d, dx=dx, dy=dy):
-                for kind in range(2):
-                    halo_copy(number, d, kind, h_src, rim, pos).wait_recv()
-                (_, nr, r1), (_, nc, c1) = side(dx, tx), side(dy, ty)
-                for row in range(r1, r1 + nr):
-                    for col in range(c1, c1 + nc):
-                        prepare(row, col, rim[row, col])
-                        prepare_pos(row, col, pos[row, col])
-
+        each_direction(lambda d, kind: halo_copy(number, d, kind).wait_recv(), -1)
+
+        def rim_body(t, carry):
+            row, col = t // ey, lax.rem(t, ey)
+            inside = (row >= 1) & (row <= tx) & (col >= 1) & (col <= ty)
+            near_x = ((row >= 1) | (gx > 0)) & ((row <= tx) | (gx < nx - 1))
+            near_y = ((col >= 1) | (gy > 0)) & ((col <= ty) | (gy < ny - 1))
+
+            @pl.when(near_x & near_y & jnp.logical_not(inside))
+            def _():
+                prepare(row, col, rim_both[number, row, col], pos_both[number, row, col], False)
+
+            return carry
+
+        lax.fori_loop(0, ex * ey, rim_body, 0)
         rest = [(n, n + 1) if n + 1 < slot_count else (n,) for n in range(1, slot_count, 2)]
 
         def body(i, carry):
             a, b = i // ty, lax.rem(i, ty)
             here = near_ref[own_of(i)]
             score_slots(i, rest, own_of(i), q_ref[i], here, slot_reader(i), work, s_ref, falloff)
-            finish(i, a, b, *finish_tile(
-                i, own_of(i), h_src[a, b], here, rows_of(noise, a, b, 0.0), scale, slot_reader(i),
-                slot_count, work, s_ref, mixing, out_w))
+            updated, moved, force = finish_tile(
+                i, own_of(i), h_both[number, a, b], here, rows_of(noise_both.at[number], a, b, 0.0),
+                scale, slot_reader(i), slot_count, work, s_ref, mixing, out_w)
+
+            @pl.when(number == 0)
+            def _():
+                finish_first(i, a, b, updated, moved, force)
+
+            @pl.when(number == 1)
+            def _():
+                finish_second(i, a, b, updated, moved, force)
+
+            for done in (tiles // groups, tiles - 1):
+                @pl.when((number == 0) & (i == done - 1))
+                def _(done=done):
+                    after_first(done)
+
             return carry
 
-        for first, last in zip(cuts[:-1], cuts[1:]):
-            lax.fori_loop(first, last, body, 0)
-            after_cut(last)
-        for d, (dx, dy) in enumerate(DIRECTIONS):
-            @pl.when(has(dx, dy))
-            def _(d=d):
-                for kind in range(2):
-                    halo_copy(number, d, kind, h_src, rim, pos).wait_send()
+        lax.fori_loop(0, tiles, body, 0)
+
+        @pl.when(number == 0)
+        def _():
+            after_first(tiles)
+            exchange_end()
+
+        each_direction(lambda d, kind: halo_copy(number, d, kind).wait_send(), 1)
 
     def swap_copy(phase, part, k, src, dst):
         return pltpu.make_async_remote_copy(
@@ -367,51 +398,32 @@
             moved_out[0, c, a, pl.ds(b, 1), :] = moved[c : c + 1]
             force_out[0, c, a, pl.ds(b, 1), :] = force[c : c + 1]
 
-    grid = [(a, b) for a in range(tx) for b in range(ty)]
-    half_tiles = tiles // groups
-    for a, b in grid:
-        pos1[a + 1, b + 1] = rows_of(p_in, a, b, 1.0)
-    for a, b in grid[:half_tiles]:
-        prepare(a + 1, b + 1, h_in[0, a, b])
+    def place_pos(number, a, b, rows):
+        rows = rows + [jnp.full((1, beads), 1.0, jnp.float32), jnp.zeros((4, beads), jnp.float32)]
+        pos_both[number, a + 1, b + 1] = jnp.concatenate(rows, axis=0)
+
+    def exchange_end():
+        for part in range(groups + 1):
+            for k in range(1, reps):
+                second_copy(part, k).wait_recv()
+        for a in range(tx):
+            for b in range(ty):
+                at = [c * tiles + a * ty + b for c in range(3)]
+                place_pos(1, a, b, [trade_p[r // per, r % per : r % per + 1, :] for r in at])
+
+    for a in range(tx):
+        for b in range(ty):
+            place_pos(0, a, b, [p_in[0, c, a, b : b + 1, :] for c in range(3)])
     mine_p[...] = jnp.zeros_like(mine_p)
-
     columns = 1 + jnp.minimum(gx, 1) + jnp.minimum(nx - 1 - gx, 1)
     lines = 1 + jnp.minimum(gy, 1) + jnp.minimum(ny - 1 - gy, 1)
     pl.semaphore_wait(barrier, reps - 2 + columns * lines)
 
-    for kind in range(2):
-        start_halo(0, kind, h_in.at[0], rim1, pos1)
-    for a, b in grid[half_tiles:]:
-        prepare(a + 1, b + 1, h_in[0, a, b])
-    for a, b in grid:
-        prepare_pos(a + 1, b + 1, rows_of(p_in, a, b, 1.0))
-    cuts = (0, half_tiles, tiles - 1, tiles)
-    step(0, h_in.at[0], rim1, pos1, noise1, finish_first, cuts, after_first)
-
-    def arrive(part):
-        for k in range(1, reps):
-            second_copy(part, k).wait_recv()
-
-    arrive(0)
-    for a, b in grid[:half_tiles]:
-        prepare(a + 1, b + 1, trade_h[a, b])
-    arrive(groups)
-    for a, b in grid:
-        rows = []
-        for c in range(3):
-            row = c * tiles + a * ty + b
-            rows.append(trade_p[row // per, row % per : row % per + 1, :])
-        rows.append(jnp.full((1, beads), 1.0, jnp.float32))
-        rows.append(jnp.zeros((4, beads), jnp.float32))
-        pos2[a + 1, b + 1] = jnp.concatenate(rows, axis=0)
-    start_halo(1, 1, trade_h, rim2, pos2)
-    arrive(1)
-    start_halo(1, 0, trade_h, rim2, pos2)
-    for a, b in grid[half_tiles:]:
-        prepare(a + 1, b + 1, trade_h[a, b])
-    for a, b in grid:
-        prepare_pos(a + 1, b + 1, pos2[a + 1, b + 1])
-    step(1, trade_h, rim2, pos2, noise2, finish_second, (0, tiles), lambda done: None)
+    def steps(number, carry):
+        step(number)
+        return carry
+
+    lax.fori_loop(0, 2, steps, 0)
     for part in range(groups + 1):
         for k in range(1, reps):
             first_copy(part, k).wait_send()
@@ -470,8 +482,14 @@
         in_specs=[pl.BlockSpec(memory_space=pltpu.HBM)] * OPERANDS,
         out_specs=(vmem, vmem, vmem),
         scratch_shapes=[
+            pltpu.VMEM((2, tx, ty, beads, feats), bf16),
+            pltpu.VMEM(particle_locations_all.shape, f32),
+            pltpu.VMEM((2, 3, tx, ty, beads), f32),
+        ]
+        + [
             (pltpu.SMEM if n in (4, 5, 6, 7, 12, 13) else pltpu.VMEM)(x.shape, x.dtype)
             for n, x in enumerate(operands)
+            if n >= 4
         ]
         + [
             pltpu.SemaphoreType.DMA((OPERANDS,)),
@@ -480,10 +498,8 @@
             pltpu.VMEM((ext, 8, beads), f32),
             pltpu.VMEM((tiles, beads, feats), bf16),
             pltpu.VMEM((tiles, heads * beads, slot_count * beads), bf16),
-            pltpu.VMEM((tx + 2, ty + 2, beads, feats), bf16),
-            pltpu.VMEM((tx + 2, ty + 2, beads, feats), bf16),
-            pltpu.VMEM((tx + 2, ty + 2, 8, beads), f32),
-            pltpu.VMEM((tx + 2, ty + 2, 8, beads), f32),
+            pltpu.VMEM((2, tx + 2, ty + 2, beads, feats), bf16),
+            pltpu.VMEM((2, tx + 2, ty + 2, 8, beads), f32),
             pltpu.VMEM((groups, reps, piece, feats), bf16),
             pltpu.VMEM((reps, per, beads), f32),
             pltpu.VMEM((reps, piece, feats), bf16),
@@ -491,7 +507,6 @@
             pltpu.VMEM((reps, per, beads), f32),
             pltpu.VMEM((groups, reps, piece, feats), bf16),
             pltpu.VMEM((reps, per, beads), f32),
-            pltpu.VMEM((tx, ty, beads, feats), bf16),
             pltpu.VMEM((reps, per, beads), f32),
             pltpu.SemaphoreType.DMA((2, len(DIRECTIONS), 2)),
             pltpu.SemaphoreType.DMA((2, len(DIRECTIONS), 2)),

time: 44.9 us -> 48.6 us (1.082)
  Pallas kernels: 40.5 us -> 44.2 us
    pallas_call x1, Pallas kernels: 40.5 us -> 44.2 us  [per_device(): pl.pallas_call(functools.partial(window_kernel, (reps, nx, ny)), out_shap...]
where the time goes in v4:
time: 48.6 us; the launch traced here: 48.4 us
  Pallas kernels  44.2 us (91%)
  local copies, waits for them, and re-layouts  2.87 us (6%)
  between operations  1.3 us (3%)
    pallas_call x1, Pallas kernels, per_device(): pl.pallas_call(functools.partial(window_kernel, (reps, nx, ny)), out_shap...  44.2 us
    unnamed x7, local copies, waits for them, and re-layouts  2.87 us

profile of v4, /device:TPU:0, one launch (start us, length us, event | category | flops | bytes accessed | tf_op | source)
XLA Modules:
  0.0 48.4 jit_solution(4811123254330431897)
XLA Ops:
  1.3 44.2 %shard_map.157 = (bf16[1,2,2,128,128]{4,3,2,1,0:T(8,128)(2,1)}, f32[1,3,2,2,128]{4,3,2,1,0:T(2,128)}, f32[1,3,2,2,128]{4,3,2,1,0:T(2,128)}) custom-call(bf16[1,2,2,128,128]{4,3,2,1,0:T(8,128)(2,1)} %refs_0_.1, f32[1,3,2,2,128]{4,3,2,1,0:T(2,128)} %refs_1_.1, f32[1,3,2,2,128]{4,3,2,1,0:T(2,128)} %refs_2_.1, f32[1,3,2,2,128]{4,3,2,1,0:T(2,128)} %refs_3_.1, ...), custom_call_target="tpu_custom_call" | custom-call | tf_op jit(solution)/shard_map/pallas_call | solution.py:475
  45.5 0.0 copy-start.1
  45.5 1.6 %copy.21 = bf16[1,2,2,128,128]{4,3,2,1,0:T(8,128)(2,1)} copy(bf16[1,2,2,128,128]{4,3,2,1,0:T(8,128)(2,1)} %get-tuple-element.6) | data formatting | bytes 262144
  47.1 0.0 copy-done.1
  47.1 0.0 copy-start
  47.1 0.6 %copy.22 = f32[1,3,2,2,128]{4,3,2,1,0:T(2,128)} copy(f32[1,3,2,2,128]{4,3,2,1,0:T(2,128)S(1)} %copy-done.1) | data formatting | bytes 12288
  47.7 0.1 copy-done
  47.8 0.6 %copy.23 = f32[1,3,2,2,128]{4,3,2,1,0:T(2,128)} copy(f32[1,3,2,2,128]{4,3,2,1,0:T(2,128)S(1)} %copy-done) | data formatting | bytes 12288
Async XLA Ops:
  45.5 1.6 %copy-start.1 = (f32[1,3,2,2,128]{4,3,2,1,0:T(2,128)S(1)}, f32[1,3,2,2,128]{4,3,2,1,0:T(2,128)}, u32[]{:S(2)}) copy-start(f32[1,3,2,2,128]{4,3,2,1,0:T(2,128)} %get-tuple-element.7) | copy-start | bytes 18436
  47.1 0.7 %copy-start = (f32[1,3,2,2,128]{4,3,2,1,0:T(2,128)S(1)}, f32[1,3,2,2,128]{4,3,2,1,0:T(2,128)}, u32[]{:S(2)}) copy-start(f32[1,3,2,2,128]{4,3,2,1,0:T(2,128)} %get-tuple-element.8) | copy-start | bytes 18436

commit v5 on v3

--- a/solution.py
+++ b/solution.py
@@ -79,7 +79,7 @@
         keys = join([k_ref[w] for w in where], 0)
         logits = lax.dot_general(
             stacked, keys, (((1,), (1,)), ((), ())), preferred_element_type=jnp.float32
-        ).astype(jnp.bfloat16)
+        )
         near = join([near_ref[w] for w in where], 1)
         occupied = join([jnp.full((1, beads), v, jnp.float32) for v in present], 1)
         for r in chunks:
@@ -96,7 +96,7 @@
             for e in range(heads):
                 start = r * heads + e * CHUNK
                 half = logits[start : start + CHUNK]
-                act = half + half * jnp.tanh(half)
+                act = (half + half * jnp.tanh(half)).astype(jnp.bfloat16)
                 decay = jnp.exp2((squared * rates[e]).astype(jnp.bfloat16))
                 s_ref[i, start : start + CHUNK, part[0] * beads : (part[-1] + 1) * beads] = act * (
                     window * decay
@@ -257,7 +257,7 @@
                         s_ref, falloff)
             return carry
 
-        lax.fori_loop(0, tiles, self_body, 0)
+        lax.fori_loop(0, tiles, self_body, 0, unroll=True)
         for d, (dx, dy) in enumerate(DIRECTIONS):
             @pl.when(has(-dx, -dy))
             def _(d=d, dx=dx, dy=dy):
@@ -281,7 +281,7 @@
             return carry
 
         for first, last in zip(cuts[:-1], cuts[1:]):
-            lax.fori_loop(first, last, body, 0)
+            lax.fori_loop(first, last, body, 0, unroll=2 if (last - first) % 2 == 0 else 1)
             after_cut(last)
         for d, (dx, dy) in enumerate(DIRECTIONS):
             @pl.when(has(dx, dy))

time: 44.9 us -> 45.5 us (1.013)
  Pallas kernels: 40.5 us -> 41.2 us
    pallas_call x1, Pallas kernels: 40.5 us -> 41.2 us  [per_device(): pl.pallas_call(functools.partial(window_kernel, (reps, nx, ny)), out_shap...]
where the time goes in v5:
time: 45.5 us; the launch traced here: 45.3 us
  Pallas kernels  41.2 us (91%)
  local copies, waits for them, and re-layouts  2.87 us (6%)
  between operations  1.3 us (3%)
    pallas_call x1, Pallas kernels, per_device(): pl.pallas_call(functools.partial(window_kernel, (reps, nx, ny)), out_shap...  41.2 us
    unnamed x7, local copies, waits for them, and re-layouts  2.87 us

profile of v5, /device:TPU:0, one launch (start us, length us, event | category | flops | bytes accessed | tf_op | source)
XLA Modules:
  0.0 45.3 jit_solution(5765266681058265635)
XLA Ops:
  1.3 41.2 %shard_map.157 = (bf16[1,2,2,128,128]{4,3,2,1,0:T(8,128)(2,1)}, f32[1,3,2,2,128]{4,3,2,1,0:T(2,128)}, f32[1,3,2,2,128]{4,3,2,1,0:T(2,128)}) custom-call(bf16[1,2,2,128,128]{4,3,2,1,0:T(8,128)(2,1)} %refs_0_.1, f32[1,3,2,2,128]{4,3,2,1,0:T(2,128)} %refs_1_.1, f32[1,3,2,2,128]{4,3,2,1,0:T(2,128)} %refs_2_.1, f32[1,3,2,2,128]{4,3,2,1,0:T(2,128)} %refs_3_.1, ...), custom_call_target="tpu_custom_call" | custom-call | tf_op jit(solution)/shard_map/pallas_call | solution.py:463
  42.5 0.0 copy-start.1
  42.5 1.6 %copy.21 = bf16[1,2,2,128,128]{4,3,2,1,0:T(8,128)(2,1)} copy(bf16[1,2,2,128,128]{4,3,2,1,0:T(8,128)(2,1)} %get-tuple-element.6) | data formatting | bytes 262144
  44.0 0.0 copy-done.1
  44.0 0.0 copy-start
  44.0 0.6 %copy.22 = f32[1,3,2,2,128]{4,3,2,1,0:T(2,128)} copy(f32[1,3,2,2,128]{4,3,2,1,0:T(2,128)S(1)} %copy-done.1) | data formatting | bytes 12288
  44.6 0.1 copy-done
  44.7 0.6 %copy.23 = f32[1,3,2,2,128]{4,3,2,1,0:T(2,128)} copy(f32[1,3,2,2,128]{4,3,2,1,0:T(2,128)S(1)} %copy-done) | data formatting | bytes 12288
Async XLA Ops:
  42.5 1.6 %copy-start.1 = (f32[1,3,2,2,128]{4,3,2,1,0:T(2,128)S(1)}, f32[1,3,2,2,128]{4,3,2,1,0:T(2,128)}, u32[]{:S(2)}) copy-start(f32[1,3,2,2,128]{4,3,2,1,0:T(2,128)} %get-tuple-element.7) | copy-start | bytes 18436
  44.0 0.7 %copy-start = (f32[1,3,2,2,128]{4,3,2,1,0:T(2,128)S(1)}, f32[1,3,2,2,128]{4,3,2,1,0:T(2,128)}, u32[]{:S(2)}) copy-start(f32[1,3,2,2,128]{4,3,2,1,0:T(2,128)} %get-tuple-element.8) | copy-start | bytes 18436
